TPU v7x, 512 devices: a whole 4x8x8 slice. The times are simulated.
512 devices in a mesh: dp: 16 (over y_lo, x), expert: 32 (over z, y_hi, core).
Axes of the slice: x: 4, y: 8 (y_hi: 2, y_lo: 4; y = y_hi * 4 + y_lo), z: 8, core: 2. Of those that a mesh axis runs over, the one named last changes fastest.
Arguments:
- tokens: bfloat16 [6144, 4096], P('expert', 'dp'), may hold values from -6 to 6
- cotangent: bfloat16 [6144, 4096], P('expert', 'dp'), may hold values from -4 to 4
- expert_ids: int32 [6144, 2], P('expert'), may hold values from 0 to 31, all different within a row; in each aligned block of 192 rows (0 to 191, 192 to 383, ...) at most 24 rows name the same one
- gate_values: float32 [6144, 2], P('expert'), may hold values from 0.1 to 0.9
- gate_up_weight: bfloat16 [32, 4096, 2048], P('expert', 'dp'), may hold values from -0.09375 to 0.09375
- down_weight: bfloat16 [32, 1024, 4096], P('expert', None, 'dp'), may hold values from -0.1875 to 0.1875
Outputs:
- layer_output: bfloat16 [6144, 4096], P('expert', 'dp')
- token_gradient: bfloat16 [6144, 4096], P('expert', 'dp')
- gate_gradient: float32 [6144, 2], P('expert')
- gate_up_gradient: bfloat16 [32, 4096, 2048], P('expert', 'dp')
- down_gradient: bfloat16 [32, 1024, 4096], P('expert', None, 'dp')
Inputs may be any that keep to these rules, and one draw needn't show every extreme that they name: `expert_ids`: each token names two different experts. In each aligned block of 192 tokens no expert is named more than 24 times, a bound that some block reaches.
All inputs are finite; a program needn't handle non-finite values. Where the computation divides by a largest or mean magnitude, that divisor is 1e-20 or more.
Results may differ from a plain program's by a relative error of at most 0.04.
Values may be sent and summed in bfloat16 or wider, within the bound.
A program may use at most 64 MiB of HBM per device.

v0:
```python
import jax
import jax.numpy as jnp
from jax import lax
from jax.sharding import PartitionSpec as P

HB = 128


def hadamard_signs(table_order):
    row_bits = jnp.arange(table_order, dtype=jnp.int32)[:, None]
    col_bits = jnp.arange(table_order, dtype=jnp.int32)[None, :]
    parity = jnp.zeros((table_order, table_order), jnp.int32)
    for bit_index in range(table_order.bit_length() - 1):
        common_bits = jnp.bitwise_and(
            jnp.right_shift(row_bits, bit_index), jnp.right_shift(col_bits, bit_index)
        )
        parity = parity + jnp.bitwise_and(common_bits, 1)
    return (1 - 2 * jnp.bitwise_and(parity, 1)).astype(jnp.float32)


def rotate_blocks(values, sign_table):
    count_rows, features = values.shape
    blocks = values.astype(jnp.float32).reshape(count_rows, features // HB, HB)
    turned = jnp.einsum(
        "nbi,ij->nbj", blocks, sign_table, precision=lax.Precision.HIGHEST
    ) * HB ** (-0.5)
    return turned.reshape(count_rows, features)


def quantize(turned):
    count_rows, features = turned.shape
    blocks = turned.reshape(count_rows, features // HB, HB)
    block_scale = (jnp.max(jnp.abs(blocks), axis=2) + 1e-06).astype(jnp.bfloat16)
    coded_rows = (blocks / block_scale.astype(jnp.float32)[:, :, None]).astype(jnp.bfloat16)
    return (coded_rows.reshape(count_rows, features), block_scale)


def restore(coded_rows, block_scale):
    count_rows, features = coded_rows.shape
    blocks = coded_rows.astype(jnp.float32).reshape(count_rows, features // HB, HB)
    restored = (blocks * block_scale.astype(jnp.float32)[:, :, None]).astype(jnp.bfloat16)
    return restored.reshape(count_rows, features)


def slot_positions(block_ids, experts):
    flat_ids = block_ids.reshape(-1)
    onehot = (flat_ids[:, None] == jnp.arange(experts, dtype=jnp.int32)[None, :]).astype(jnp.int32)
    earlier = jnp.cumsum(onehot, axis=0) - onehot
    return jnp.sum(onehot * earlier, axis=1).reshape(block_ids.shape)


def unrotate_pairs(picked, sign_table):
    count_rows, pair_count, features = picked.shape
    blocks = picked.astype(jnp.float32).reshape(count_rows, pair_count, features // HB, HB)
    turned = jnp.einsum(
        "nkbi,ij->nkbj", blocks, sign_table, precision=lax.Precision.HIGHEST
    ) * HB ** (-0.5)
    return jnp.sum(turned, axis=1).reshape(count_rows, features)


def activation_grad(hidden_grad, gate_pre, up_pre, sigmoid_gate, activated):
    gate_part = hidden_grad * up_pre * sigmoid_gate * (1.0 + gate_pre * (1.0 - sigmoid_gate))
    up_part = hidden_grad * activated
    return jnp.concatenate([gate_part, up_part], axis=1).astype(jnp.bfloat16)


def per_device(tokens, cotangent, expert_ids, gate_values, gate_up_weight, down_weight):
    experts = lax.axis_size("expert")
    tok_rows, width_local = tokens.shape
    capacity = 4 * tok_rows // experts
    total_rows = experts * capacity
    gate_up = gate_up_weight[0]
    down_matrix = down_weight[0]
    hidden_width = down_matrix.shape[0]
    sign_table = hadamard_signs(HB)
    coded_rows, block_scale = quantize(rotate_blocks(tokens, sign_table))
    slot_rank = slot_positions(expert_ids, experts)
    target_row = expert_ids * capacity + slot_rank
    slot_index = jnp.arange(total_rows, dtype=jnp.int32)[:, None]
    first_hit = target_row[:, 0][None, :] == slot_index
    second_hit = target_row[:, 1][None, :] == slot_index
    placement = jnp.logical_or(first_hit, second_hit).astype(jnp.bfloat16)
    sent_codes = jnp.dot(placement, coded_rows, preferred_element_type=jnp.float32).astype(
        jnp.bfloat16
    )
    sent_scales = jnp.dot(placement, block_scale, preferred_element_type=jnp.float32).astype(
        jnp.bfloat16
    )
    slot_weight = jnp.sum(
        jnp.where(first_hit, gate_values[:, 0][None, :], 0.0)
        + jnp.where(second_hit, gate_values[:, 1][None, :], 0.0),
        axis=1,
    )
    picked_cot = jnp.dot(placement, cotangent, preferred_element_type=jnp.float32)
    sent_grads = (slot_weight[:, None] * picked_cot).astype(jnp.bfloat16)
    arrived = (
        lax.all_to_all(
            sent_codes.reshape(experts, capacity, width_local),
            "expert",
            split_axis=0,
            concat_axis=0,
            tiled=True,
        ),
        lax.all_to_all(
            sent_scales.reshape(experts, capacity, -1),
            "expert",
            split_axis=0,
            concat_axis=0,
            tiled=True,
        ),
        lax.all_to_all(
            sent_grads.reshape(experts, capacity, width_local),
            "expert",
            split_axis=0,
            concat_axis=0,
            tiled=True,
        ),
    )
    restored = restore(
        arrived[0].reshape(total_rows, width_local), arrived[1].reshape(total_rows, -1)
    )
    expert_grad = arrived[2].reshape(total_rows, width_local)
    pre_act = lax.psum(
        jnp.dot(restored, gate_up, preferred_element_type=jnp.float32).astype(jnp.bfloat16), "dp"
    ).astype(jnp.float32)
    gate_pre = pre_act[:, :hidden_width]
    up_pre = pre_act[:, hidden_width:]
    sigmoid_gate = jax.nn.sigmoid(gate_pre)
    activated = gate_pre * sigmoid_gate
    hidden = (activated * up_pre).astype(jnp.bfloat16)
    expert_out = jnp.dot(hidden, down_matrix, preferred_element_type=jnp.float32).astype(
        jnp.bfloat16
    )
    down_total = lax.dot_general(
        hidden, expert_grad, (((0,), (0,)), ((), ())), preferred_element_type=jnp.float32
    )
    partial_grad = lax.dot_general(
        expert_grad, down_matrix, (((1,), (1,)), ((), ())), preferred_element_type=jnp.float32
    )
    hidden_grad = lax.psum(partial_grad.astype(jnp.bfloat16), "dp").astype(jnp.float32)
    act_grad = activation_grad(hidden_grad, gate_pre, up_pre, sigmoid_gate, activated)
    gate_up_total = lax.dot_general(
        restored, act_grad, (((0,), (0,)), ((), ())), preferred_element_type=jnp.float32
    )
    input_grad = lax.dot_general(
        act_grad, gate_up, (((1,), (1,)), ((), ())), preferred_element_type=jnp.float32
    ).astype(jnp.bfloat16)
    returned = lax.all_to_all(
        expert_out.reshape(experts, capacity, width_local),
        "expert",
        split_axis=0,
        concat_axis=0,
        tiled=True,
    ).reshape(total_rows, width_local)
    picked_out = jnp.take(returned, target_row, axis=0)
    layer_output = jnp.sum(gate_values[:, :, None] * picked_out.astype(jnp.float32), axis=1).astype(
        jnp.bfloat16
    )
    gate_partial = jnp.sum(
        cotangent.astype(jnp.float32)[:, None, :] * picked_out.astype(jnp.float32), axis=2
    )
    gate_gradient = lax.psum(gate_partial, "dp")
    grads_home = lax.all_to_all(
        input_grad.reshape(experts, capacity, width_local),
        "expert",
        split_axis=0,
        concat_axis=0,
        tiled=True,
    ).reshape(total_rows, width_local)
    token_gradient = unrotate_pairs(jnp.take(grads_home, target_row, axis=0), sign_table).astype(
        jnp.bfloat16
    )
    return (
        layer_output,
        token_gradient,
        gate_gradient,
        gate_up_total.astype(jnp.bfloat16)[None],
        down_total.astype(jnp.bfloat16)[None],
    )


def solution(mesh):
    return jax.shard_map(
        per_device,
        mesh=mesh,
        in_specs=(
            P("expert", "dp"),
            P("expert", "dp"),
            P("expert", None),
            P("expert", None),
            P("expert", "dp", None),
            P("expert", None, "dp"),
        ),
        out_specs=(
            P("expert", "dp"),
            P("expert", "dp"),
            P("expert", None),
            P("expert", "dp", None),
            P("expert", None, "dp"),
        ),
        check_vma=False,
    )
```

profile of v0, /device:TPU:32, one launch (start us, length us, event | category | flops | bytes accessed | tf_op | source)
XLA Modules:
  0.0 414.6 jit_solution(147480089178044492)
XLA Ops:
  7.2 0.0 copy-start
  7.2 0.0 copy-start.5
  7.2 0.0 copy-start.4
  7.2 0.9 copy.88
  8.1 0.1 eq.59
  8.3 0.1 eq.55
  8.4 0.9 reduce-window.6
  9.3 0.2 slice_reduce_fusion
  9.6 0.1 fusion.44
  9.7 0.1 reshape.185
  9.8 0.1 copy.91
  9.9 0.7 compare_and_fusion
  10.6 1.4 abs_reduce_fusion
  12.0 0.3 convolution_convert_fusion.6
  12.4 0.1 reshape.189
  12.5 0.6 copy.95
  13.1 15.8 %all-to-all-start.1 = ((bf16[32,24,2]{1,2,0:T(2,128)(2,1)}), bf16[32,24,2]{1,2,0:T(2,128)(2,1)S(1)}, u32[]{:S(2)}, u32[]{:S(2)}) async-start(bf16[32,24,2]{1,2,0:T(2,128)(2,1)} %copy.95), calls=%async_computation.1 | async-start | bytes 32768 | tf_op jit(solution)/shard_map/all_to_all | solution.py:104
  29.0 1.3 convolution_convert_fusion.5
  30.2 5.8 %all-to-all-done.1 = bf16[32,24,2]{1,2,0:T(2,128)(2,1)S(1)} async-done(((bf16[32,24,2]{1,2,0:T(2,128)(2,1)}), bf16[32,24,2]{1,2,0:T(2,128)(2,1)S(1)}, u32[]{:S(2)}, u32[]{:S(2)}) %all-to-all-start.1) | async-done | bytes 3104 | tf_op jit(solution)/shard_map/all_to_all | solution.py:104
  36.0 8.8 %all-to-all-start = ((bf16[32,24,256]{2,1,0:T(8,128)(2,1)}), bf16[32,24,256]{2,1,0:T(8,128)(2,1)S(1)}, u32[]{:S(2)}, u32[]{:S(2)}) async-start(bf16[32,24,256]{2,1,0:T(8,128)(2,1)} %bitcast.5), calls=%async_computation | async-start | bytes 786432 | tf_op jit(solution)/shard_map/all_to_all | solution.py:97
  44.8 0.0 copy-done.5
  44.8 0.2 add_reduce_fusion
  45.0 0.0 copy-done.4
  45.0 1.3 fusion.7
  46.3 13.5 %all-to-all-done = bf16[32,24,256]{2,1,0:T(8,128)(2,1)S(1)} async-done(((bf16[32,24,256]{2,1,0:T(8,128)(2,1)}), bf16[32,24,256]{2,1,0:T(8,128)(2,1)S(1)}, u32[]{:S(2)}, u32[]{:S(2)}) %all-to-all-start) | async-done | bytes 393248 | tf_op jit(solution)/shard_map/all_to_all | solution.py:97
  59.8 7.4 %all-to-all-start.3 = ((bf16[32,24,256]{2,1,0:T(8,128)(2,1)}), bf16[32,24,256]{2,1,0:T(8,128)(2,1)S(1)}, u32[]{:S(2)}, u32[]{:S(2)}) async-start(bf16[32,24,256]{2,1,0:T(8,128)(2,1)} %bitcast.13), calls=%async_computation.3 | async-start | bytes 786432 | tf_op jit(solution)/shard_map/all_to_all | solution.py:111
  67.2 0.0 all-reduce.3.cloned.1.call-start
  67.2 0.1 copy.96
  67.3 0.3 copy.106
  67.6 0.4 reshape.197
  68.0 1.0 multiply_convert_fusion.1
  69.0 13.0 %all-to-all-done.3 = bf16[32,24,256]{2,1,0:T(8,128)(2,1)S(1)} async-done(((bf16[32,24,256]{2,1,0:T(8,128)(2,1)}), bf16[32,24,256]{2,1,0:T(8,128)(2,1)S(1)}, u32[]{:S(2)}, u32[]{:S(2)}) %all-to-all-start.3) | async-done | bytes 393248 | tf_op jit(solution)/shard_map/all_to_all | solution.py:111
  81.9 2.9 convolution_convert_fusion.2
  84.8 0.0 copy-done
  84.8 2.7 convolution_convert_fusion
  87.5 0.0 all-reduce.3.cloned.1.call-update
  87.5 182.4 %all-reduce.3.cloned.1.call-done = (bf16[768,2048]{1,0:T(8,128)(2,1)}, bf16[768,1024]{1,0:T(8,128)(2,1)}) async-done(((bf16[768,2048]{1,0:T(8,128)(2,1)}, bf16[768,1024]{1,0:T(8,128)(2,1)}), (bf16[768,2048]{1,0:T(8,128)(2,1)}, bf16[768,1024]{1,0:T(8,128)(2,1)})) %all-reduce.3.cloned.1.call-update) | async-done | bytes 4718608 | tf_op jit(solution)/shard_map/psum | solution.py:123
  269.9 2.8 convert_element_type.149
  272.7 0.0 copy-start.3
  272.8 3.2 fusion.2
  276.0 1.1 copy-done.1
  277.1 1.3 convolution_convert_fusion.4
  278.5 12.9 %all-to-all-start.2 = ((bf16[32,24,256]{2,1,0:T(8,128)(2,1)}), bf16[32,24,256]{2,1,0:T(8,128)(2,1)S(1)}, u32[]{:S(2)}, u32[]{:S(2)}) async-start(bf16[32,24,256]{2,1,0:T(8,128)(2,1)} %bitcast.9), calls=%async_computation.2 | async-start | bytes 786432 | tf_op jit(solution)/shard_map/all_to_all | solution.py:148
  291.4 0.1 copy.87
  291.5 0.2 copy.92
  291.7 0.1 copy.99
  291.8 0.1 reshape.220
  292.0 1.0 mul.103
  292.9 0.1 fusion.13
  293.0 3.7 fusion.8
  296.7 9.4 %all-to-all-done.2 = bf16[32,24,256]{2,1,0:T(8,128)(2,1)S(1)} async-done(((bf16[32,24,256]{2,1,0:T(8,128)(2,1)}), bf16[32,24,256]{2,1,0:T(8,128)(2,1)S(1)}, u32[]{:S(2)}, u32[]{:S(2)}) %all-to-all-start.2) | async-done | bytes 393248 | tf_op jit(solution)/shard_map/all_to_all | solution.py:148
  306.0 7.6 %all-to-all-start.4 = ((bf16[32,24,256]{2,1,0:T(8,128)(2,1)}), bf16[32,24,256]{2,1,0:T(8,128)(2,1)S(1)}, u32[]{:S(2)}, u32[]{:S(2)}) async-start(bf16[32,24,256]{2,1,0:T(8,128)(2,1)} %bitcast.15), calls=%async_computation.4 | async-start | bytes 786432 | tf_op jit(solution)/shard_map/all_to_all | solution.py:163
  313.7 2.8 fusion.9
  316.5 3.9 fusion.5
  320.3 2.0 gather_fusion
  322.4 0.1 reshape.223
  322.5 1.9 fusion.18
  324.4 79.4 %psum.23 = f32[192,2]{1,0:T(8,128)S(1)} all-reduce(f32[192,2]{1,0:T(8,128)S(1)} %get-tuple-element.26), channel_id=1, replica_groups=mesh['dp'=16,'expert'=32] {'dp'}, use_global_device_ids=true, to_apply=%region_10.12 | all-reduce | flops 384 | bytes 3072 | tf_op jit(solution)/shard_map/psum | solution.py:162
  403.8 0.7 copy.104
  404.4 0.0 all-to-all-done.4
  404.4 2.0 gather_fusion.1
  406.5 0.1 reshape.227
  406.6 0.5 fusion.10
  407.1 0.7 copy_bitcast_fusion
  (16 shorter events, 0.1 us)
Async XLA Ops:
  7.2 77.6 %copy-start = (bf16[1,256,2048]{2,1,0:T(8,128)(2,1)S(1)}, bf16[1,256,2048]{2,1,0:T(8,128)(2,1)}, u32[]{:S(2)}) copy-start(bf16[1,256,2048]{2,1,0:T(8,128)(2,1)} %param.12) | copy-start | bytes 3145732
  7.2 37.6 %copy-start.5 = (f32[192,2]{0,1:T(2,128)S(1)}, f32[192,2]{0,1:T(2,128)}, u32[]{:S(2)}) copy-start(f32[192,2]{0,1:T(2,128)} %param.11) | copy-start | bytes 4612
  7.2 37.8 %copy-start.4 = (bf16[192,256]{1,0:T(8,128)(2,1)S(1)}, bf16[192,256]{1,0:T(8,128)(2,1)}, u32[]{:S(2)}) copy-start(bf16[192,256]{1,0:T(8,128)(2,1)} %param.9) | copy-start | bytes 294916
  13.1 22.9 %all-to-all-start.1 = ((bf16[32,24,2]{1,2,0:T(2,128)(2,1)}), bf16[32,24,2]{1,2,0:T(2,128)(2,1)S(1)}, u32[]{:S(2)}, u32[]{:S(2)}) async-start(bf16[32,24,2]{1,2,0:T(2,128)(2,1)} %copy.95), calls=%async_computation.1 | async-start | bytes 32768 | tf_op jit(solution)/shard_map/all_to_all | solution.py:104
  36.0 23.8 %all-to-all-start = ((bf16[32,24,256]{2,1,0:T(8,128)(2,1)}), bf16[32,24,256]{2,1,0:T(8,128)(2,1)S(1)}, u32[]{:S(2)}, u32[]{:S(2)}) async-start(bf16[32,24,256]{2,1,0:T(8,128)(2,1)} %bitcast.5), calls=%async_computation | async-start | bytes 786432 | tf_op jit(solution)/shard_map/all_to_all | solution.py:97
  59.8 22.1 %all-to-all-start.3 = ((bf16[32,24,256]{2,1,0:T(8,128)(2,1)}), bf16[32,24,256]{2,1,0:T(8,128)(2,1)S(1)}, u32[]{:S(2)}, u32[]{:S(2)}) async-start(bf16[32,24,256]{2,1,0:T(8,128)(2,1)} %bitcast.13), calls=%async_computation.3 | async-start | bytes 786432 | tf_op jit(solution)/shard_map/all_to_all | solution.py:111
  67.2 202.7 %all-reduce.3.cloned.1.call-start = ((), (), s32[]{:S(2)}) async-start(), calls=%async_computation.5 | async-start | bytes 9437184 | tf_op jit(solution)/shard_map/psum | solution.py:123
  269.9 2.9 copy-start.2
  272.7 4.4 %copy-start.3 = (bf16[1,1024,256]{2,1,0:T(8,128)(2,1)S(1)}, bf16[1,1024,256]{2,1,0:T(8,128)(2,1)}, u32[]{:S(2)}) copy-start(bf16[1,1024,256]{2,1,0:T(8,128)(2,1)} %param.13) | copy-start | bytes 1572868
  276.0 1.1 copy-start.1
  278.5 27.6 %all-to-all-start.2 = ((bf16[32,24,256]{2,1,0:T(8,128)(2,1)}), bf16[32,24,256]{2,1,0:T(8,128)(2,1)S(1)}, u32[]{:S(2)}, u32[]{:S(2)}) async-start(bf16[32,24,256]{2,1,0:T(8,128)(2,1)} %bitcast.9), calls=%async_computation.2 | async-start | bytes 786432 | tf_op jit(solution)/shard_map/all_to_all | solution.py:148
  306.0 98.4 %all-to-all-start.4 = ((bf16[32,24,256]{2,1,0:T(8,128)(2,1)}), bf16[32,24,256]{2,1,0:T(8,128)(2,1)S(1)}, u32[]{:S(2)}, u32[]{:S(2)}) async-start(bf16[32,24,256]{2,1,0:T(8,128)(2,1)} %bitcast.15), calls=%async_computation.4 | async-start | bytes 786432 | tf_op jit(solution)/shard_map/all_to_all | solution.py:163
Sparse Core Ops, SparseCore 0:
  87.6 182.1 all-reduce.2
where the time goes:
time: 415 us
  waiting for transfers between devices  224 us (54%)
  blocking collectives  79.4 us (19%)
  starting transfers between devices  52.5 us (13%)
  matrix products  22 us (5%)
  between operations  14.4 us (3%)
  local copies, waits for them, and re-layouts  11.3 us (3%)
  other arithmetic  11 us (3%)
    psum x1, waiting for transfers between devices, per_device(): lax.psum(jnp.dot(restored, gate_up, preferred_element_type=jnp.float32).a...  182 us
    psum x1, blocking collectives, per_device(): gate_gradient = lax.psum(gate_partial, 'dp')  79.4 us
    all_to_all x1, starting transfers between devices, per_device(): lax.all_to_all(sent_scales.reshape(experts, capacity, -1), 'expert', spli...  15.8 us
    all_to_all x1, waiting for transfers between devices, per_device(): lax.all_to_all(sent_codes.reshape(experts, capacity, width_local), 'exper...  13.5 us
    all_to_all x1, waiting for transfers between devices, per_device(): lax.all_to_all(sent_grads.reshape(experts, capacity, width_local), 'exper...  13 us
    all_to_all x1, starting transfers between devices, per_device(): lax.all_to_all(expert_out.reshape(experts, capacity, width_local), 'exper...  12.9 us
    all_to_all x1, waiting for transfers between devices, per_device(): lax.all_to_all(expert_out.reshape(experts, capacity, width_local), 'exper...  9.35 us
    all_to_all x1, starting transfers between devices, per_device(): lax.all_to_all(sent_codes.reshape(experts, capacity, width_local), 'exper...  8.77 us
  transfers between devices with their start and end apart: 6, of which 5 were waited for; matrix products, arithmetic and copies ran while one was open for 5% of the time, Pallas kernels for 0%

commit v1 on v0

v1 whole, which is shorter than its diff:
```python
import functools

import jax
import jax.numpy as jnp
import numpy as np
from jax import lax
from jax.experimental import pallas as pl
from jax.experimental.pallas import tpu as pltpu
from jax.sharding import PartitionSpec as P

HB = 128
MESH = pl.DeviceIdType.MESH
BF = jnp.bfloat16
F32 = jnp.float32

NX, NY = 4, 4
NE = 32
CAP = 24
ROWS = NE * CAP
TOK = 192
KD = 256
FF = 1024
UC = 512
NU = 6
SH = 48


def sign_blocks():
    idx = np.arange(KD)
    common = (idx[:, None] & idx[None, :]) & (HB - 1)
    parity = np.zeros((KD, KD), np.int64)
    for bit in range(7):
        parity += (common >> bit) & 1
    signs = 1 - 2 * (parity & 1)
    return np.where((idx[:, None] // HB) == (idx[None, :] // HB), signs, 0)


def dot_nn(a, b):
    return lax.dot_general(a, b, (((1,), (0,)), ((), ())), preferred_element_type=F32)


def dot_nt(a, b):
    return lax.dot_general(a, b, (((1,), (1,)), ((), ())), preferred_element_type=F32)


def dot_tn(a, b):
    return lax.dot_general(a, b, (((0,), (0,)), ((), ())), preferred_element_type=F32)


def kernel(
    tok_ref, cot_ref, ids_ref, gate_ref, w_ref, dn_ref, sign_ref,
    lo_ref, tg_ref, gg_ref, gu_ref, dg_ref,
    send_x, send_g, send_o, send_i, got_x, got_g, got_o, got_i,
    xs, gs, xt, gt, hits,
    part, r1, r2, q, yr, gu_keep, full, acc_o, acc_i, gx, gy,
    s_a2a, r_a2a, s_x1, s_x2, s_y, s_ya, s_xa1, s_xa2,
    m_x1, m_x2, m_y, m_ya, m_xa1, m_xa2, s_gate, m_gate,
):
    dp = lax.axis_index("dp")
    me = lax.axis_index("expert")
    x = lax.rem(dp, NX)
    y = lax.div(dp, NX)
    xr, xo, xl = lax.rem(x + 1, NX), lax.rem(x + 2, NX), lax.rem(x + 3, NX)

    def at_x(other):
        return (y * NX + other, me)

    def at_y(other):
        return (other * NX + x, me)

    def send(src, dst, send_sem, recv_sem, device):
        pltpu.make_async_remote_copy(
            src_ref=src, dst_ref=dst, send_sem=send_sem, recv_sem=recv_sem,
            device_id=device, device_id_type=MESH,
        ).start()

    def wait_for(sem, ref):
        pltpu.make_async_copy(ref, ref, sem).wait()

    barrier = pltpu.get_barrier_semaphore()

    def greet(i, _):
        pl.semaphore_signal(
            barrier, inc=1, device_id=(dp, lax.rem(me + i, NE)), device_id_type=MESH
        )
        return 0

    lax.fori_loop(1, NE, greet, 0)
    for other in (xr, xo, xl):
        pl.semaphore_signal(barrier, inc=1, device_id=at_x(other), device_id_type=MESH)
    for j in (1, 2, 3):
        pl.semaphore_signal(
            barrier, inc=1, device_id=at_y(lax.rem(y + j, NY)), device_id_type=MESH
        )

    turned = dot_nn(tok_ref[...], sign_ref[...]) * (HB ** -0.5)
    pieces = []
    for b in range(KD // HB):
        block = turned[:, b * HB:(b + 1) * HB]
        top = jnp.max(jnp.abs(block), axis=1, keepdims=True) + 1e-06
        scale = jnp.broadcast_to(top, block.shape).astype(BF).astype(F32)
        coded = (block / scale).astype(BF)
        pieces.append((coded.astype(F32) * scale).astype(BF))
    restored = jnp.concatenate(pieces, axis=1)

    lanes = lax.broadcasted_iota(jnp.int32, (TOK, 128), 1)
    one0 = jnp.where(ids_ref[:, 0:1] == lanes, 1.0, 0.0)
    one1 = jnp.where(ids_ref[:, 1:2] == lanes, 1.0, 0.0)
    below = jnp.where(
        lax.broadcasted_iota(jnp.int32, (TOK, TOK), 0)
        > lax.broadcasted_iota(jnp.int32, (TOK, TOK), 1),
        1.0, 0.0,
    ).astype(BF)
    earlier = dot_nn(below, (one0 + one1).astype(BF))
    row_lanes = lax.broadcasted_iota(jnp.int32, (TOK, ROWS), 1)
    for k, one in enumerate((one0, one1)):
        rank = jnp.sum(one * earlier, axis=1, keepdims=True).astype(jnp.int32)
        target = ids_ref[:, k:k + 1] * CAP + rank
        hits[k] = jnp.where(target == row_lanes, 1.0, 0.0).astype(BF)

    both = (hits[0].astype(F32) + hits[1].astype(F32)).astype(BF)
    send_x[...] = dot_tn(both, restored).reshape(NE, CAP, KD).astype(BF)

    pl.semaphore_wait(barrier, NE - 1 + 6)

    def scatter(src, dst, n):
        def one_peer(i, _):
            peer = lax.rem(me + i, NE)
            send(src.at[peer], dst.at[me], s_a2a.at[n], r_a2a.at[n], (dp, peer))
            return 0

        lax.fori_loop(1, NE, one_peer, 0)
        dst[me] = src[me]

    def arrived(dst, n):
        wait_for(r_a2a.at[n], dst.at[pl.ds(0, NE - 1)])
        return dst[...].astype(F32).reshape(ROWS, KD).astype(BF)

    scatter(send_x, got_x, 0)

    cot = cot_ref[...].astype(F32)
    w0 = (gate_ref[:, 0:1] * cot).astype(BF)
    w1 = (gate_ref[:, 1:2] * cot).astype(BF)
    sent = dot_tn(hits[0], w0) + dot_tn(hits[1], w1)
    send_g[...] = sent.reshape(NE, CAP, KD).astype(BF)
    scatter(send_g, got_g, 1)

    def x1_send(u):
        send(part.at[u, pl.ds(4 * xo, 2)], r1.at[u, 0], s_x1, m_x1.at[u], at_x(xr))
        send(part.at[u, pl.ds(4 * xo + 2, 2)], r1.at[u, 1], s_x1, m_x1.at[u], at_x(xl))
        send(part.at[u, pl.ds(4 * xr + 2, 2)], r2.at[u, 0, pl.ds(2, 2)], s_x2, m_x2.at[u], at_x(xr))
        send(part.at[u, pl.ds(4 * xl, 2)], r2.at[u, 1, pl.ds(0, 2)], s_x2, m_x2.at[u], at_x(xl))

    def x1_pass(u):
        wait_for(m_x1.at[u], r1.at[u])
        lower = pl.ds(4 * xr, 2)
        part[u, lower] = (part[u, lower].astype(F32) + r1[u, 0].astype(F32)).astype(BF)
        send(part.at[u, lower], r2.at[u, 0, pl.ds(0, 2)], s_x2, m_x2.at[u], at_x(xr))
        upper = pl.ds(4 * xl + 2, 2)
        part[u, upper] = (part[u, upper].astype(F32) + r1[u, 1].astype(F32)).astype(BF)
        send(part.at[u, upper], r2.at[u, 1, pl.ds(2, 2)], s_x2, m_x2.at[u], at_x(xl))

    def x2_sum(u):
        wait_for(m_x2.at[u], r2.at[u])
        own = part[u, pl.ds(4 * x, 4)].astype(F32)
        q[u] = (own + r2[u, 0].astype(F32) + r2[u, 1].astype(F32)).astype(BF)
        for j in (1, 2, 3):
            other = lax.rem(y + j, NY)
            send(q.at[u, other], yr.at[u, j - 1], s_y, m_y.at[u], at_y(other))

    def y_sum(u):
        wait_for(m_y.at[u], yr.at[u])
        total = q[u, y].astype(F32) + yr[u, 0].astype(F32)
        return total + yr[u, 1].astype(F32) + yr[u, 2].astype(F32)

    home = 4 * x + y

    def ya_send(a):
        for j in (1, 2, 3):
            send(full.at[a, home], full.at[a, home], s_ya, m_ya.at[a], at_y(lax.rem(y + j, NY)))

    def xa1_send(a):
        wait_for(m_ya.at[a], yr.at[a])
        mine = pl.ds(4 * x, 4)
        for other in (xr, xl):
            send(full.at[a, mine], full.at[a, mine], s_xa1, m_xa1.at[a], at_x(other))

    def xa1_pass(a):
        wait_for(m_xa1.at[a], r2.at[a])
        lower, upper = pl.ds(4 * xl, 2), pl.ds(4 * xr + 2, 2)
        send(full.at[a, lower], full.at[a, lower], s_xa2, m_xa2.at[a], at_x(xr))
        send(full.at[a, upper], full.at[a, upper], s_xa2, m_xa2.at[a], at_x(xl))

    def gathered(a):
        wait_for(m_xa2.at[a], r1.at[a])

    def forward_part(c):
        for half in range(2):
            cols = slice(half * FF + 256 * c, half * FF + 256 * c + 256)
            out = dot_nn(xs[...], w_ref[:, cols]).astype(BF)
            part[c, :, :, 256 * half:256 * half + 256] = out.reshape(16, SH, 256)

    def backward_part(d):
        out = dot_nt(gs[...], dn_ref[UC * d:UC * d + UC, :]).astype(BF)
        part[4 + d] = out.reshape(16, SH, UC)

    def make_hidden(c):
        total = y_sum(c)
        gu_keep[c] = total
        gate, up = total[:, :256], total[:, 256:]
        hidden = (gate * jax.nn.sigmoid(gate)) * up
        a, half = c // 2, c % 2
        full[a, home, :, 256 * half:256 * half + 256] = hidden.astype(BF)

    def make_act(d):
        total = y_sum(4 + d)
        for half in range(2):
            c = 2 * d + half
            grad = total[:, 256 * half:256 * half + 256]
            gate, up = gu_keep[c, :, :256], gu_keep[c, :, 256:]
            sig = jax.nn.sigmoid(gate)
            cols = slice(256 * half, 256 * half + 256)
            full[2 + 2 * d, home, :, cols] = (grad * up * sig * (1.0 + gate * (1.0 - sig))).astype(BF)
            full[3 + 2 * d, home, :, cols] = (grad * (gate * sig)).astype(BF)

    def whole(a):
        return full[a].reshape(ROWS, UC)

    def use_hidden(a):
        gathered(a)
        rows = slice(UC * a, UC * a + UC)
        out = dot_nn(whole(a), dn_ref[rows, :])
        if a == 0:
            acc_o[...] = out
        else:
            send_o[...] = (acc_o[...] + out).reshape(NE, CAP, KD).astype(BF)
            scatter(send_o, got_o, 2)

    def hidden_weights(a):
        rows = slice(UC * a, UC * a + UC)
        dg_ref[rows, :] = dot_nn(gt[...], whole(a)).T.astype(BF)

    act_columns = {2: 0, 3: FF, 4: UC, 5: FF + UC}

    def use_act(a):
        gathered(a)
        cols = slice(act_columns[a], act_columns[a] + UC)
        out = dot_nt(whole(a), w_ref[:, cols])
        if a == 2:
            acc_i[...] = out
        elif a < 5:
            acc_i[...] += out
        else:
            send_i[...] = (acc_i[...] + out).reshape(NE, CAP, KD).astype(BF)
            scatter(send_i, got_i, 3)

    def act_weights(a):
        cols = slice(act_columns[a], act_columns[a] + UC)
        gu_ref[:, cols] = dot_nn(xt[...], whole(a)).astype(BF)

    xs[...] = arrived(got_x, 0)
    for c in range(4):
        forward_part(c)
        x1_send(c)
    x1_pass(0)
    x1_pass(1)
    gs[...] = arrived(got_g, 1)
    for d in range(2):
        backward_part(d)
        x1_send(4 + d)
    x1_pass(2)
    x2_sum(0)
    x1_pass(3)
    x2_sum(1)
    xt[...] = xs[...].T
    gt[...] = gs[...].T
    make_hidden(0)
    x1_pass(4)
    x2_sum(2)
    make_hidden(1)
    ya_send(0)
    x1_pass(5)
    x2_sum(3)
    make_hidden(2)
    xa1_send(0)
    x2_sum(4)
    make_hidden(3)
    ya_send(1)
    x2_sum(5)
    make_act(0)
    ya_send(2)
    ya_send(3)
    xa1_send(1)
    xa1_pass(0)
    make_act(1)
    ya_send(4)
    ya_send(5)
    xa1_send(2)
    xa1_send(3)
    xa1_pass(1)
    use_hidden(0)
    xa1_send(4)
    xa1_send(5)
    use_hidden(1)
    xa1_pass(2)
    hidden_weights(0)
    xa1_pass(3)
    hidden_weights(1)
    use_act(2)
    act_weights(2)
    xa1_pass(4)
    use_act(3)
    xa1_pass(5)
    act_weights(3)

    back = arrived(got_o, 2)
    p0, p1 = dot_nn(hits[0], back), dot_nn(hits[1], back)
    lo_ref[...] = (gate_ref[:, 0:1] * p0 + gate_ref[:, 1:2] * p1).astype(BF)
    ones = jnp.ones((8, KD), F32)

    def lane_sums(values):
        return lax.dot_general(
            ones, values, (((1,), (1,)), ((), ())),
            precision=lax.Precision.HIGHEST, preferred_element_type=F32,
        )

    cot_again = cot_ref[...].astype(F32)
    first = lax.broadcasted_iota(jnp.int32, (8, TOK), 0) == 0
    gx[x] = jnp.where(first, lane_sums(cot_again * p0), lane_sums(cot_again * p1))
    for j, other in enumerate((xr, xo, xl)):
        send(gx.at[x], gx.at[x], s_gate.at[0, j], m_gate.at[0, x], at_x(other))
    use_act(4)
    act_weights(4)
    for other in (xr, xo, xl):
        wait_for(m_gate.at[0, other], gx.at[other])
    gy[y] = (gx[0] + gx[1]) + (gx[2] + gx[3])
    for j in (1, 2, 3):
        send(gy.at[y], gy.at[y], s_gate.at[1, j - 1], m_gate.at[1, y], at_y(lax.rem(y + j, NY)))
    use_act(5)
    act_weights(5)
    for j in (1, 2, 3):
        other = lax.rem(y + j, NY)
        wait_for(m_gate.at[1, other], gy.at[other])
    gg_ref[...] = (gy[0] + gy[1]) + (gy[2] + gy[3])

    back = arrived(got_i, 3)
    pair = dot_nn(hits[0], back) + dot_nn(hits[1], back)
    high = pair.astype(BF)
    low = (pair - high.astype(F32)).astype(BF)
    signs = sign_ref[...]
    tg_ref[...] = ((dot_nn(high, signs) + dot_nn(low, signs)) * (HB ** -0.5)).astype(BF)

    for n, buf in enumerate((send_x, send_g, send_o, send_i)):
        wait_for(s_a2a.at[n], buf.at[pl.ds(0, NE - 1)])
    wait_for(s_x1, r1)
    wait_for(s_x2, r2)
    wait_for(s_y, yr)
    wait_for(s_ya, yr)
    wait_for(s_xa1, r2)
    wait_for(s_xa2, r1)
    for j in range(3):
        wait_for(s_gate.at[0, j], gx.at[0])
        wait_for(s_gate.at[1, j], gy.at[0])


def per_device(tokens, cotangent, expert_ids, gate_values, gate_up_weight, down_weight):
    vmem = pl.BlockSpec(memory_space=pltpu.VMEM)
    slabs = pltpu.VMEM((NE, CAP, KD), BF)
    dma = pltpu.SemaphoreType.DMA
    lo, tg, gg, gu, dg = pl.pallas_call(
        kernel,
        out_shape=(
            jax.ShapeDtypeStruct((TOK, KD), BF),
            jax.ShapeDtypeStruct((TOK, KD), BF),
            jax.ShapeDtypeStruct((8, TOK), F32),
            jax.ShapeDtypeStruct((KD, 2 * FF), BF),
            jax.ShapeDtypeStruct((FF, KD), BF),
        ),
        in_specs=[vmem] * 7,
        out_specs=[vmem] * 5,
        scratch_shapes=[
            slabs, slabs, slabs, slabs, slabs, slabs, slabs, slabs,
            pltpu.VMEM((ROWS, KD), BF), pltpu.VMEM((ROWS, KD), BF),
            pltpu.VMEM((KD, ROWS), BF), pltpu.VMEM((KD, ROWS), BF),
            pltpu.VMEM((2, TOK, ROWS), BF),
            pltpu.VMEM((NU, 16, SH, UC), BF),
            pltpu.VMEM((NU, 2, 2, SH, UC), BF),
            pltpu.VMEM((NU, 2, 4, SH, UC), BF),
            pltpu.VMEM((NU, 4, SH, UC), BF),
            pltpu.VMEM((NU, 3, SH, UC), BF),
            pltpu.VMEM((4, SH, UC), F32),
            pltpu.VMEM((NU, 16, SH, UC), BF),
            pltpu.VMEM((ROWS, KD), F32), pltpu.VMEM((ROWS, KD), F32),
            pltpu.VMEM((NX, 8, TOK), F32), pltpu.VMEM((NY, 8, TOK), F32),
            dma((4,)), dma((4,)),
            dma, dma, dma, dma, dma, dma,
            dma((NU,)), dma((NU,)), dma((NU,)), dma((NU,)), dma((NU,)), dma((NU,)),
            dma((2, 3)), dma((2, 4)),
        ],
        compiler_params=pltpu.CompilerParams(
            collective_id=0, has_side_effects=True, vmem_limit_bytes=56 * 1024 * 1024
        ),
        cost_estimate=pl.CostEstimate(
            flops=2 * ROWS * KD * 9 * FF, bytes_accessed=6 * 1024 * 1024, transcendentals=ROWS * FF
        ),
    )(
        tokens, cotangent, expert_ids, gate_values, gate_up_weight[0], down_weight[0],
        jnp.asarray(sign_blocks(), BF),
    )
    return lo, tg, gg[:2].T, gu[None], dg[None]


def solution(mesh):
    return jax.shard_map(
        per_device,
        mesh=mesh,
        in_specs=(
            P("expert", "dp"),
            P("expert", "dp"),
            P("expert", None),
            P("expert", None),
            P("expert", "dp", None),
            P("expert", None, "dp"),
        ),
        out_specs=(
            P("expert", "dp"),
            P("expert", "dp"),
            P("expert", None),
            P("expert", "dp", None),
            P("expert", None, "dp"),
        ),
        check_vma=False,
    )
```

time: 415 us -> 160 us (0.39)
  the two profiles are of different devices: /device:TPU:32 before, /device:TPU:1 now
where the time goes in v1:
time: 160 us; the launch traced here: 158 us
  Pallas kernels  148 us (92%)
  local copies, waits for them, and re-layouts  8.87 us (6%)
    pallas_call x1, Pallas kernels, per_device(): pl.pallas_call(kernel, out_shape=(jax.ShapeDtypeStruct((TOK, KD), BF), ja...  148 us
    unnamed x14, local copies, waits for them, and re-layouts  7.59 us

profile of v1, /device:TPU:1, one launch (start us, length us, event | category | flops | bytes accessed | tf_op | source)
XLA Modules:
  0.0 157.8 jit_solution(11083506208320129966)
XLA Ops:
  0.6 0.0 copy-start.2
  0.6 0.7 copy-done.2
  1.3 0.0 copy-start.3
  1.3 0.8 copy.12.ids_ref
  2.1 0.0 copy-done.3
  2.1 0.8 copy.13.gate_ref
  2.9 148.3 %shard_map.110 = (bf16[192,256]{1,0:T(8,128)(2,1)}, bf16[192,256]{1,0:T(8,128)(2,1)}, f32[8,192]{1,0:T(8,128)}, bf16[256,2048]{1,0:T(8,128)(2,1)}, bf16[1024,256]{1,0:T(8,128)(2,1)}) custom-call(bf16[192,256]{1,0:T(8,128)(2,1)} %tok_ref.1, bf16[192,256]{1,0:T(8,128)(2,1)} %cot_ref.1, s32[192,2]{1,0:T(8,128)} %copy.12.ids_ref, f32[192,2]{1,0:T(8,128)} %copy.13.gate_ref, ...), custom_call_target="tpu_custom_call" | custom-call | flops 3623878656 | bytes 6291456 | tf_op jit(solution)/shard_map/pallas_call | solution.py:370
  151.1 1.3 slice_bitcast_fusion
  152.4 0.0 copy-start.1
  152.4 1.6 copy.18
  154.0 0.0 copy-done.1
  154.0 0.6 copy.19
  154.6 0.0 copy-start
  154.6 2.4 %copy.20 = bf16[1,256,2048]{2,1,0:T(8,128)(2,1)} copy(bf16[1,256,2048]{2,1,0:T(8,128)(2,1)} %bitcast.6) | data formatting | bytes 2097152
  157.0 0.0 copy-done
  157.0 0.8 copy.21
Async XLA Ops:
  0.6 0.7 copy-start.2
  1.3 0.8 copy-start.3
  152.4 1.6 copy-start.1
  154.6 2.4 %copy-start = (bf16[1024,256]{1,0:T(8,128)(2,1)S(1)}, bf16[1024,256]{1,0:T(8,128)(2,1)}, u32[]{:S(2)}) copy-start(bf16[1024,256]{1,0:T(8,128)(2,1)} %get-tuple-element.14) | copy-start | bytes 1572868

commit v2 on v1

v2 whole, which is shorter than its diff:
```python
import functools

import jax
import jax.numpy as jnp
from jax import lax
from jax.experimental import pallas as pl
from jax.experimental.pallas import tpu as pltpu
from jax.sharding import PartitionSpec as P

HB = 128
MESH = pl.DeviceIdType.MESH
BF = jnp.bfloat16
F32 = jnp.float32

NX, NY = 4, 4
NE = 32
CAP = 24
ROWS = NE * CAP
TOK = 192
KD = 256
FF = 1024
UC = 512
NU = 6
NH, NA = 2, 3
SH = 48
AR = SH // NA


def dot_nn(a, b):
    return lax.dot_general(a, b, (((1,), (0,)), ((), ())), preferred_element_type=F32)


def dot_nt(a, b):
    return lax.dot_general(a, b, (((1,), (1,)), ((), ())), preferred_element_type=F32)


def dot_tn(a, b):
    return lax.dot_general(a, b, (((0,), (0,)), ((), ())), preferred_element_type=F32)


def signs_of_block():
    common = jnp.bitwise_and(
        lax.broadcasted_iota(jnp.int32, (HB, HB), 0), lax.broadcasted_iota(jnp.int32, (HB, HB), 1)
    )
    for shift in (4, 2, 1):
        common = jnp.bitwise_xor(common, jnp.right_shift(common, shift))
    return (1 - 2 * jnp.bitwise_and(common, 1)).astype(F32).astype(BF)


def kernel(
    tok_ref, cot_ref, ids_ref, gate_ref, w_hbm, dn_hbm,
    lo_ref, tg_ref, gg_ref, gu_hbm, dg_hbm,
    w_ref, dn_ref, gu_ref, dg_ref, gu_acc, signs,
    send_x, send_g, send_o, send_i, got_x, got_g, got_o, got_i,
    xs, gs, xt, gt, hits, hits_t,
    part, r1, r2, q, yr, gu_keep, full, fa, acc_o, ig, gx, gy,
    s_local, s_a2a, r_a2a, s_x1, s_x2, s_y, m_x1, m_x2, m_y,
    s_ya, s_xa1, s_xa2, m_ya, m_xa1, m_xa2, s_gate, m_gate,
):
    dp = lax.axis_index("dp")
    me = lax.axis_index("expert")
    x = lax.rem(dp, NX)
    y = lax.div(dp, NX)
    xr, xo, xl = lax.rem(x + 1, NX), lax.rem(x + 2, NX), lax.rem(x + 3, NX)

    def at_x(other):
        return (y * NX + other, me)

    def at_y(other):
        return (other * NX + x, me)

    def send(src, dst, send_sem, recv_sem, device):
        pltpu.make_async_remote_copy(
            src_ref=src, dst_ref=dst, send_sem=send_sem, recv_sem=recv_sem,
            device_id=device, device_id_type=MESH,
        ).start()

    def wait_for(sem, ref):
        pltpu.make_async_copy(ref, ref, sem).wait()

    barrier = pltpu.get_barrier_semaphore()

    def greet(i, _):
        pl.semaphore_signal(
            barrier, inc=1, device_id=(dp, lax.rem(me + i, NE)), device_id_type=MESH
        )
        return 0

    lax.fori_loop(1, NE, greet, 0)
    for other in (xr, xo, xl):
        pl.semaphore_signal(barrier, inc=1, device_id=at_x(other), device_id_type=MESH)
    for j in (1, 2, 3):
        pl.semaphore_signal(
            barrier, inc=1, device_id=at_y(lax.rem(y + j, NY)), device_id_type=MESH
        )
    fetch_w = pltpu.make_async_copy(w_hbm, w_ref, s_local.at[0])
    fetch_dn = pltpu.make_async_copy(dn_hbm, dn_ref, s_local.at[1])
    fetch_w.start()
    fetch_dn.start()

    places = lax.broadcasted_iota(jnp.int32, (NE, TOK), 0)
    one0 = jnp.where(ids_ref[0:1, :] == places, 1.0, 0.0)
    one1 = jnp.where(ids_ref[1:2, :] == places, 1.0, 0.0)
    before = jnp.where(
        lax.broadcasted_iota(jnp.int32, (TOK, TOK), 0)
        < lax.broadcasted_iota(jnp.int32, (TOK, TOK), 1),
        1.0, 0.0,
    ).astype(BF)
    earlier = dot_nn((one0 + one1).astype(BF), before)
    targets = []
    for k, one in enumerate((one0, one1)):
        rank = jnp.sum(one * earlier, axis=0, keepdims=True)
        targets.append(ids_ref[k:k + 1, :].astype(F32) * CAP + rank)
    rows = lax.broadcasted_iota(jnp.int32, (ROWS, TOK), 0)
    hit0 = targets[0].astype(jnp.int32) == rows
    hit1 = targets[1].astype(jnp.int32) == rows
    hits_t[0] = jnp.where(hit0, 1.0, 0.0).astype(BF)
    hits_t[1] = jnp.where(hit1, 1.0, 0.0).astype(BF)
    both = jnp.where(jnp.logical_or(hit0, hit1), 1.0, 0.0).astype(BF)

    signs[...] = signs_of_block()
    pieces = []
    for b in range(KD // HB):
        block = dot_nn(tok_ref[:, b * HB:(b + 1) * HB], signs[...]) * (HB ** -0.5)
        top = jnp.max(jnp.abs(block), axis=1, keepdims=True) + 1e-06
        scale = jnp.broadcast_to(top, block.shape).astype(BF).astype(F32)
        coded = (block / scale).astype(BF)
        pieces.append((coded.astype(F32) * scale).astype(BF))
    restored = jnp.concatenate(pieces, axis=1)
    send_x[...] = dot_nn(both, restored).reshape(NE, CAP, KD).astype(BF)

    pl.semaphore_wait(barrier, NE - 1 + 6)

    def scatter(src, dst, n):
        def one_peer(i, _):
            peer = lax.rem(me + i, NE)
            send(src.at[peer], dst.at[me], s_a2a.at[n], r_a2a.at[n], (dp, peer))
            return 0

        lax.fori_loop(1, NE, one_peer, 0)
        dst[me] = src[me]

    def arrived(dst, n):
        wait_for(r_a2a.at[n], got_x.at[pl.ds(0, NE - 1)])
        return dst[...].astype(F32).reshape(ROWS, KD).astype(BF)

    scatter(send_x, got_x, 0)

    small = jnp.concatenate(
        [targets[0], targets[1], gate_ref[...], jnp.zeros((4, TOK), F32)], axis=0
    )
    columns = jnp.concatenate([small, jnp.zeros((8, 256 - TOK), F32)], axis=1).T[:TOK]
    gate0, gate1 = columns[:, 2:3], columns[:, 3:4]
    cot = cot_ref[...].astype(F32)
    sent = dot_nn(hits_t[0], (gate0 * cot).astype(BF)) + dot_nn(hits_t[1], (gate1 * cot).astype(BF))
    send_g[...] = sent.reshape(NE, CAP, KD).astype(BF)
    scatter(send_g, got_g, 1)
    row_lanes = lax.broadcasted_iota(jnp.int32, (TOK, ROWS), 1)
    for k in range(2):
        hits[k] = jnp.where(columns[:, k:k + 1].astype(jnp.int32) == row_lanes, 1.0, 0.0).astype(BF)

    def x1(u):
        send(part.at[u, pl.ds(4 * xo, 2)], r1.at[u, 0], s_x1, m_x1.at[u], at_x(xr))
        send(part.at[u, pl.ds(4 * xo + 2, 2)], r1.at[u, 1], s_x1, m_x1.at[u], at_x(xl))

    def x2_plain(u):
        send(part.at[u, pl.ds(4 * xr + 2, 2)], r2.at[u, 0, pl.ds(2, 2)], s_x2, m_x2.at[u], at_x(xr))
        send(part.at[u, pl.ds(4 * xl, 2)], r2.at[u, 1, pl.ds(0, 2)], s_x2, m_x2.at[u], at_x(xl))

    def x2_added(u):
        wait_for(m_x1.at[u], r1.at[u])
        lower = pl.ds(4 * xr, 2)
        part[u, lower] = (part[u, lower].astype(F32) + r1[u, 0].astype(F32)).astype(BF)
        send(part.at[u, lower], r2.at[u, 0, pl.ds(0, 2)], s_x2, m_x2.at[u], at_x(xr))
        upper = pl.ds(4 * xl + 2, 2)
        part[u, upper] = (part[u, upper].astype(F32) + r1[u, 1].astype(F32)).astype(BF)
        send(part.at[u, upper], r2.at[u, 1, pl.ds(2, 2)], s_x2, m_x2.at[u], at_x(xl))

    def x2_sum(u):
        wait_for(m_x2.at[u], r2.at[u])
        own = part[u, pl.ds(4 * x, 4)].astype(F32)
        q[u] = (own + r2[u, 0].astype(F32) + r2[u, 1].astype(F32)).astype(BF)
        for j in (2, 1, 3):
            other = lax.rem(y + j, NY)
            send(q.at[u, other], yr.at[u, j - 1], s_y, m_y.at[u], at_y(other))

    def y_sum(u):
        wait_for(m_y.at[u], yr.at[u])
        total = q[u, y].astype(F32) + yr[u, 0].astype(F32)
        return total + yr[u, 1].astype(F32) + yr[u, 2].astype(F32)

    home = 4 * x + y

    def unit(a):
        return full.at[a] if a < NH else fa.at[a - NH]

    def ya(a):
        block = unit(a).at[home]
        for j in (2, 1, 3):
            send(block, block, s_ya.at[a], m_ya.at[a], at_y(lax.rem(y + j, NY)))

    def xa1(a):
        wait_for(m_ya.at[a], unit(a).at[pl.ds(0, 3)])
        mine = unit(a).at[pl.ds(4 * x, 4)]
        for other in (xr, xl):
            send(mine, mine, s_xa1.at[a], m_xa1.at[a], at_x(other))

    def xa2(a):
        wait_for(m_xa1.at[a], unit(a).at[pl.ds(0, 8)])
        lower, upper = unit(a).at[pl.ds(4 * xl, 2)], unit(a).at[pl.ds(4 * xr + 2, 2)]
        send(lower, lower, s_xa2.at[a], m_xa2.at[a], at_x(xr))
        send(upper, upper, s_xa2.at[a], m_xa2.at[a], at_x(xl))

    def gathered(a):
        wait_for(m_xa2.at[a], unit(a).at[pl.ds(0, 4)])

    def forward_part(c):
        left = xs[...].reshape(ROWS, KD)
        for half in range(2):
            cols = slice(half * FF + 256 * c, half * FF + 256 * c + 256)
            out = dot_nn(left, w_ref[:, cols]).astype(BF)
            part[c, :, :, 256 * half:256 * half + 256] = out.reshape(16, SH, 256)

    def backward_part(d):
        out = dot_nt(gs[...], dn_ref[UC * d:UC * d + UC, :]).astype(BF)
        part[4 + d] = out.reshape(16, SH, UC)

    def make_hidden(c):
        total = y_sum(c)
        gu_keep[c] = total
        gate, up = total[:, :256], total[:, 256:]
        hidden = (gate * jax.nn.sigmoid(gate)) * up
        a, half = c // 2, c % 2
        full[a, home, :, 256 * half:256 * half + 256] = hidden.astype(BF)

    def make_act(d):
        total = y_sum(4 + d)
        for half in range(2):
            c = 2 * d + half
            grad = total[:, 256 * half:256 * half + 256]
            gate, up = gu_keep[c, :, :256], gu_keep[c, :, 256:]
            sig = jax.nn.sigmoid(gate)
            of_gate = (grad * up * sig * (1.0 + gate * (1.0 - sig))).astype(BF)
            of_up = (grad * (gate * sig)).astype(BF)
            for r in range(NA):
                some = slice(AR * r, AR * r + AR)
                fa[r, home, :, 256 * c:256 * c + 256] = of_gate[some]
                fa[r, home, :, FF + 256 * c:FF + 256 * c + 256] = of_up[some]

    def use_hidden(a):
        gathered(a)
        out = dot_nn(full[a].reshape(ROWS, UC), dn_ref[UC * a:UC * a + UC, :])
        if a == 0:
            acc_o[...] = out
        else:
            send_o[...] = (acc_o[...] + out).reshape(NE, CAP, KD).astype(BF)
            scatter(send_o, got_o, 2)

    def hidden_weights(a):
        grads = dot_nn(gt[...], full[a].reshape(ROWS, UC))
        dg_ref[UC * a:UC * a + UC, :] = grads.T.astype(BF)

    def use_act(r):
        gathered(NH + r)
        out = dot_nt(fa[r].reshape(16 * AR, 2 * FF), w_ref[...])
        ig[:, AR * r:AR * r + AR, :] = out.reshape(16, AR, KD)

    def act_weights(r):
        for n in range(4):
            cols = slice(UC * n, UC * n + UC)
            grads = dot_nn(xt[r], fa[r, :, :, cols].reshape(16 * AR, UC))
            if r == 0:
                gu_acc[:, cols] = grads
            elif r < NA - 1:
                gu_acc[:, cols] += grads
            else:
                gu_ref[:, cols] = (gu_acc[:, cols] + grads).astype(BF)

    def scatter_half(core):
        send_i[:, core] = ig[:, CAP * core:CAP * core + CAP, :].astype(BF)
        pair, mine = lax.div(me, 2), lax.rem(me, 2)

        def one_peer(i, _):
            to = lax.rem(pair + i, NE // 2)

            @pl.when(jnp.logical_or(to != pair, mine != core))
            def _():
                send(
                    send_i.at[to, core], got_i.at[pair, mine],
                    s_a2a.at[3], r_a2a.at[3], (dp, 2 * to + core),
                )

            return 0

        lax.fori_loop(0, NE // 2, one_peer, 0)

        @pl.when(mine == core)
        def _():
            got_i[pair, core] = send_i[pair, core]

    fetch_w.wait()
    fetch_dn.wait()
    xs[...] = arrived(got_x, 0).reshape(16, SH, KD)
    forward_part(0)
    x1(0)
    x2_plain(0)
    forward_part(1)
    x1(1)
    forward_part(2)
    x2_added(0)
    x2_plain(1)
    x1(2)
    forward_part(3)
    x2_added(1)
    x2_plain(2)
    x1(3)
    x2_sum(0)
    gs[...] = arrived(got_g, 1)
    backward_part(0)
    x2_added(2)
    x2_plain(3)
    x1(4)
    x2_sum(1)
    backward_part(1)
    make_hidden(0)
    x2_added(3)
    x2_plain(4)
    x1(5)
    x2_sum(2)
    make_hidden(1)
    ya(0)
    x2_added(4)
    x2_plain(5)
    x2_sum(3)
    make_hidden(2)
    x2_added(5)
    xa1(0)
    x2_sum(4)
    make_hidden(3)
    ya(1)
    x2_sum(5)
    make_act(0)
    xa1(1)
    xa2(0)
    make_act(1)
    ya(2)
    ya(3)
    ya(4)
    for r in range(NA):
        xt[r] = xs[:, AR * r:AR * r + AR, :].reshape(16 * AR, KD).T
    gt[...] = gs[...].T
    xa2(1)
    xa1(2)
    use_hidden(0)
    xa1(3)
    use_hidden(1)
    xa1(4)
    xa2(2)
    hidden_weights(0)
    hidden_weights(1)
    put_dg = pltpu.make_async_copy(dg_ref, dg_hbm, s_local.at[2])
    put_dg.start()
    xa2(3)
    use_act(0)
    act_weights(0)
    xa2(4)

    back = arrived(got_o, 2)
    p0, p1 = dot_nn(hits[0], back), dot_nn(hits[1], back)
    lo_ref[...] = (gate0 * p0 + gate1 * p1).astype(BF)
    ones = jnp.ones((8, KD), F32)

    def lane_sums(values):
        return lax.dot_general(
            ones, values, (((1,), (1,)), ((), ())),
            precision=lax.Precision.HIGHEST, preferred_element_type=F32,
        )

    cot_again = cot_ref[...].astype(F32)
    first = lax.broadcasted_iota(jnp.int32, (8, TOK), 0) == 0
    gx[x] = jnp.where(first, lane_sums(cot_again * p0), lane_sums(cot_again * p1))
    for j, other in enumerate((xr, xo, xl)):
        send(gx.at[x], gx.at[x], s_gate.at[0, j], m_gate.at[0, x], at_x(other))
    use_act(1)
    scatter_half(0)
    act_weights(1)
    for other in (xr, xo, xl):
        wait_for(m_gate.at[0, other], gx.at[other])
    gy[y] = (gx[0] + gx[1]) + (gx[2] + gx[3])
    for j in (1, 2, 3):
        send(gy.at[y], gy.at[y], s_gate.at[1, j - 1], m_gate.at[1, y], at_y(lax.rem(y + j, NY)))
    use_act(2)
    scatter_half(1)
    act_weights(2)
    put_gu = pltpu.make_async_copy(gu_ref, gu_hbm, s_local.at[3])
    put_gu.start()
    for j in (1, 2, 3):
        other = lax.rem(y + j, NY)
        wait_for(m_gate.at[1, other], gy.at[other])
    gg_ref[...] = ((gy[0] + gy[1]) + (gy[2] + gy[3]))[0:2]

    for n, buf in enumerate((send_x, send_g, send_o)):
        wait_for(s_a2a.at[n], buf.at[pl.ds(0, NE - 1)])
    wait_for(s_x1, r1)
    wait_for(s_x2, r2)
    wait_for(s_y, yr)
    for a in range(NH + NA):
        wait_for(s_ya.at[a], unit(a).at[pl.ds(0, 3)])
        wait_for(s_xa1.at[a], unit(a).at[pl.ds(0, 8)])
        wait_for(s_xa2.at[a], unit(a).at[pl.ds(0, 4)])
    for j in range(3):
        wait_for(s_gate.at[0, j], gx.at[0])
        wait_for(s_gate.at[1, j], gy.at[0])
    put_dg.wait()

    back = arrived(got_i, 3)
    pair = dot_nn(hits[0], back) + dot_nn(hits[1], back)
    high = pair.astype(BF)
    low = (pair - high.astype(F32)).astype(BF)
    for b in range(KD // HB):
        cols = slice(b * HB, (b + 1) * HB)
        out = dot_nn(high[:, cols], signs[...]) + dot_nn(low[:, cols], signs[...])
        tg_ref[:, cols] = (out * (HB ** -0.5)).astype(BF)
    wait_for(s_a2a.at[3], send_x.at[pl.ds(0, NE - 1)])
    put_gu.wait()


def place_results(*refs):
    count = 5
    sources, targets, held = refs[:count], refs[count:2 * count], refs[2 * count:3 * count]
    s_in, s_out = refs[3 * count:]
    order = (3, 4, 0, 1, 2)
    fetch = {n: pltpu.make_async_copy(sources[n], held[n], s_in.at[n]) for n in order}
    put = {n: pltpu.make_async_copy(held[n], targets[n], s_out.at[n]) for n in order}
    for n in order:
        fetch[n].start()
    for n in order:
        fetch[n].wait()
        put[n].start()
    for n in order:
        put[n].wait()


def per_device(tokens, cotangent, expert_ids, gate_values, gate_up_weight, down_weight):
    vmem = pl.BlockSpec(memory_space=pltpu.VMEM)
    hbm = pl.BlockSpec(memory_space=pl.ANY)
    slabs = pltpu.VMEM((NE, CAP, KD), BF)
    dma = pltpu.SemaphoreType.DMA
    results = (
        jax.ShapeDtypeStruct((TOK, KD), BF),
        jax.ShapeDtypeStruct((TOK, KD), BF),
        jax.ShapeDtypeStruct((2, TOK), F32),
        jax.ShapeDtypeStruct((KD, 2 * FF), BF),
        jax.ShapeDtypeStruct((FF, KD), BF),
    )
    made = pl.pallas_call(
        kernel,
        out_shape=results,
        in_specs=[vmem] * 4 + [hbm] * 2,
        out_specs=[vmem] * 3 + [hbm] * 2,
        scratch_shapes=[
            pltpu.VMEM((KD, 2 * FF), BF), pltpu.VMEM((FF, KD), BF),
            pltpu.VMEM((KD, 2 * FF), BF), pltpu.VMEM((FF, KD), BF),
            pltpu.VMEM((KD, 2 * FF), F32), pltpu.VMEM((HB, HB), BF),
            slabs, slabs, slabs, pltpu.VMEM((NE // 2, 2, CAP, KD), BF),
            slabs, slabs, slabs, pltpu.VMEM((NE // 2, 2, CAP, KD), BF),
            pltpu.VMEM((16, SH, KD), BF), pltpu.VMEM((ROWS, KD), BF),
            pltpu.VMEM((NA, KD, 16 * AR), BF), pltpu.VMEM((KD, ROWS), BF),
            pltpu.VMEM((2, TOK, ROWS), BF), pltpu.VMEM((2, ROWS, TOK), BF),
            pltpu.VMEM((NU, 16, SH, UC), BF),
            pltpu.VMEM((NU, 2, 2, SH, UC), BF),
            pltpu.VMEM((NU, 2, 4, SH, UC), BF),
            pltpu.VMEM((NU, 4, SH, UC), BF),
            pltpu.VMEM((NU, 3, SH, UC), BF),
            pltpu.VMEM((4, SH, UC), F32),
            pltpu.VMEM((NH, 16, SH, UC), BF),
            pltpu.VMEM((NA, 16, AR, 2 * FF), BF),
            pltpu.VMEM((ROWS, KD), F32), pltpu.VMEM((16, SH, KD), F32),
            pltpu.VMEM((NX, 8, TOK), F32), pltpu.VMEM((NY, 8, TOK), F32),
            dma((4,)), dma((4,)), dma((4,)),
            dma, dma, dma, dma((NU,)), dma((NU,)), dma((NU,)),
            dma((NH + NA,)), dma((NH + NA,)), dma((NH + NA,)),
            dma((NH + NA,)), dma((NH + NA,)), dma((NH + NA,)),
            dma((2, 3)), dma((2, 4)),
        ],
        compiler_params=pltpu.CompilerParams(
            collective_id=0, has_side_effects=True, vmem_limit_bytes=56 * 1024 * 1024
        ),
        cost_estimate=pl.CostEstimate(
            flops=2 * ROWS * KD * 9 * FF, bytes_accessed=6 * 1024 * 1024, transcendentals=ROWS * FF
        ),
    )(
        tokens, cotangent, expert_ids.T, gate_values.T, gate_up_weight[0], down_weight[0],
    )
    lo, tg, gg, gu, dg = pl.pallas_call(
        place_results,
        out_shape=results,
        in_specs=[hbm] * 5,
        out_specs=[hbm] * 5,
        scratch_shapes=[pltpu.VMEM(r.shape, r.dtype) for r in results] + [dma((5,)), dma((5,))],
    )(*made)
    return lo, tg, gg.T, gu[None], dg[None]


def solution(mesh):
    return jax.shard_map(
        per_device,
        mesh=mesh,
        in_specs=(
            P("expert", "dp"),
            P("expert", "dp"),
            P("expert", None),
            P("expert", None),
            P("expert", "dp", None),
            P("expert", None, "dp"),
        ),
        out_specs=(
            P("expert", "dp"),
            P("expert", "dp"),
            P("expert", None),
            P("expert", "dp", None),
            P("expert", None, "dp"),
        ),
        check_vma=False,
    )
```

time: 160 us -> 143 us (0.89); the launches traced: 158 us -> 143 us
  local copies, waits for them, and re-layouts: 8.87 us -> 0 us
  Pallas kernels: 148 us -> 142 us
    unnamed x14 -> x0, local copies, waits for them, and re-layouts: 7.59 us -> none
    pallas_call x1 -> x2, Pallas kernels: 148 us -> 142 us  [the longest x1 140 us: per_device(): pl.pallas_call(kernel, out_shape=results, in_specs=[vmem] * 4 + [hbm] * 2...]
where the time goes in v2:
time: 143 us
  Pallas kernels  142 us (99%)
    pallas_call x1, Pallas kernels, per_device(): pl.pallas_call(kernel, out_shape=results, in_specs=[vmem] * 4 + [hbm] * 2...  140 us

profile of v2, /device:TPU:1, one launch (start us, length us, event | category | flops | bytes accessed | tf_op | source)
XLA Modules:
  0.0 142.8 jit_solution(6975705486025172158)
XLA Ops:
  0.6 139.7 %shard_map.101 = (bf16[192,256]{1,0:T(8,128)(2,1)}, bf16[192,256]{1,0:T(8,128)(2,1)}, f32[2,192]{1,0:T(2,128)}, bf16[256,2048]{1,0:T(8,128)(2,1)}, bf16[1024,256]{1,0:T(8,128)(2,1)}) custom-call(bf16[192,256]{1,0:T(8,128)(2,1)} %tok_ref.1, bf16[192,256]{1,0:T(8,128)(2,1)} %cot_ref.1, s32[2,192]{1,0:T(2,128)} %bitcast.11, f32[2,192]{1,0:T(2,128)} %bitcast.12, ...), custom_call_target="tpu_custom_call" | custom-call | flops 3623878656 | bytes 6291456 | tf_op jit(solution)/shard_map/pallas_call | solution.py:456
  140.3 2.5 %shard_map.102 = (bf16[192,256]{1,0:T(8,128)(2,1)}, bf16[192,256]{1,0:T(8,128)(2,1)}, f32[2,192]{1,0:T(2,128)}, bf16[256,2048]{1,0:T(8,128)(2,1)}, bf16[1024,256]{1,0:T(8,128)(2,1)}) custom-call(bf16[192,256]{1,0:T(8,128)(2,1)} %get-tuple-element.15.refs_0_, bf16[192,256]{1,0:T(8,128)(2,1)} %get-tuple-element.16.refs_1_, ...), custom_call_target="tpu_custom_call" | custom-call | tf_op jit(solution)/shard_map/pallas_call | solution.py:495

commit v3 on v2

v3 whole, which is shorter than its diff:
```python
import functools

import jax
import jax.numpy as jnp
from jax import lax
from jax.experimental import pallas as pl
from jax.experimental.pallas import tpu as pltpu
from jax.sharding import PartitionSpec as P

HB = 128
MESH = pl.DeviceIdType.MESH
BF = jnp.bfloat16
F32 = jnp.float32

NX, NY = 4, 4
NE = 32
CAP = 24
ROWS = NE * CAP
TOK = 192
KD = 256
FF = 1024
FX = FF // NX
NU = 4
UR = ROWS // NU
SH = UR // NY
ND = 2


def dot_nn(a, b):
    return lax.dot_general(a, b, (((1,), (0,)), ((), ())), preferred_element_type=F32)


def dot_nt(a, b):
    return lax.dot_general(a, b, (((1,), (1,)), ((), ())), preferred_element_type=F32)


def dot_tn(a, b):
    return lax.dot_general(a, b, (((0,), (0,)), ((), ())), preferred_element_type=F32)


def signs_of_block():
    common = jnp.bitwise_and(
        lax.broadcasted_iota(jnp.int32, (HB, HB), 0), lax.broadcasted_iota(jnp.int32, (HB, HB), 1)
    )
    for shift in (4, 2, 1):
        common = jnp.bitwise_xor(common, jnp.right_shift(common, shift))
    return (1 - 2 * jnp.bitwise_and(common, 1)).astype(F32).astype(BF)


def kernel(
    tok_ref, cot_ref, ids_ref, gate_ref, w_hbm, dn_hbm,
    lo_ref, tg_ref, gg_ref, gu_hbm, dg_hbm,
    w_ref, dn_ref, gu_ref, dg_ref, gu_acc, signs, wx,
    send_x, send_g, send_o, send_i, got_x, got_g, got_o, got_i,
    xg, gs, xt, gt, hits, hits_t,
    pf, fb, fc, pv, r1, r2, qv, vb, vc, gu_keep, hid, act, gx, gy,
    s_local, s_a2a, r_a2a, s_w, m_w, s_xg1, s_xg2, m_xg1, m_xg2,
    s_f1, s_f2, m_f1, m_f2, s_x1, s_x2, m_x1, m_x2, s_v1, s_v2, m_v1, m_v2,
    s_ya1, s_ya2, s_xa1, s_xa2, m_ya1, m_ya2, m_xa1, m_xa2, s_gate, m_gate,
):
    dp = lax.axis_index("dp")
    me = lax.axis_index("expert")
    x = lax.rem(dp, NX)
    y = lax.div(dp, NX)
    xr, xo, xl = lax.rem(x + 1, NX), lax.rem(x + 2, NX), lax.rem(x + 3, NX)
    y1, y2, y3 = y + 1 - 2 * lax.rem(y, 2), lax.rem(y + 2, NY), NY - 1 - y

    def at_x(other):
        return (y * NX + other, me)

    def at_y(other):
        return (other * NX + x, me)

    def send(src, dst, send_sem, recv_sem, device):
        pltpu.make_async_remote_copy(
            src_ref=src, dst_ref=dst, send_sem=send_sem, recv_sem=recv_sem,
            device_id=device, device_id_type=MESH,
        ).start()

    def wait_for(sem, ref):
        pltpu.make_async_copy(ref, ref, sem).wait()

    barrier = pltpu.get_barrier_semaphore()

    def greet(i, _):
        pl.semaphore_signal(
            barrier, inc=1, device_id=(dp, lax.rem(me + i, NE)), device_id_type=MESH
        )
        return 0

    lax.fori_loop(1, NE, greet, 0)
    for other in (xr, xo, xl):
        pl.semaphore_signal(barrier, inc=1, device_id=at_x(other), device_id_type=MESH)
    for j in (1, 2, 3):
        pl.semaphore_signal(
            barrier, inc=1, device_id=at_y(lax.rem(y + j, NY)), device_id_type=MESH
        )
    fetch_w = pltpu.make_async_copy(w_hbm, w_ref, s_local.at[0])
    fetch_dn = pltpu.make_async_copy(dn_hbm, dn_ref, s_local.at[1])
    fetch_w.start()
    fetch_dn.start()

    def own_columns(half, other):
        return w_hbm.at[:, pl.ds(pl.multiple_of(half * FF + FX * other, FX), FX)]

    keep = [
        pltpu.make_async_copy(own_columns(half, x), wx.at[x, half], s_local.at[4 + half])
        for half in range(2)
    ]
    for copy in keep:
        copy.start()

    places = lax.broadcasted_iota(jnp.int32, (NE, TOK), 0)
    one0 = jnp.where(ids_ref[0:1, :] == places, 1.0, 0.0)
    one1 = jnp.where(ids_ref[1:2, :] == places, 1.0, 0.0)
    before = jnp.where(
        lax.broadcasted_iota(jnp.int32, (TOK, TOK), 0)
        < lax.broadcasted_iota(jnp.int32, (TOK, TOK), 1),
        1.0, 0.0,
    ).astype(BF)
    earlier = dot_nn((one0 + one1).astype(BF), before)
    targets = []
    for k, one in enumerate((one0, one1)):
        rank = jnp.sum(one * earlier, axis=0, keepdims=True)
        targets.append(ids_ref[k:k + 1, :].astype(F32) * CAP + rank)
    rows = lax.broadcasted_iota(jnp.int32, (ROWS, TOK), 0)
    hit0 = targets[0].astype(jnp.int32) == rows
    hit1 = targets[1].astype(jnp.int32) == rows
    hits_t[0] = jnp.where(hit0, 1.0, 0.0).astype(BF)
    hits_t[1] = jnp.where(hit1, 1.0, 0.0).astype(BF)
    both = jnp.where(jnp.logical_or(hit0, hit1), 1.0, 0.0).astype(BF)

    pl.semaphore_wait(barrier, NE - 1 + 6)
    for half in range(2):
        for other in (xo, xr, xl):
            send(own_columns(half, other), wx.at[x, half], s_w, m_w, at_x(other))

    signs[...] = signs_of_block()
    pieces = []
    for b in range(KD // HB):
        block = dot_nn(tok_ref[:, b * HB:(b + 1) * HB], signs[...]) * (HB ** -0.5)
        top = jnp.max(jnp.abs(block), axis=1, keepdims=True) + 1e-06
        scale = jnp.broadcast_to(top, block.shape).astype(BF).astype(F32)
        coded = (block / scale).astype(BF)
        pieces.append((coded.astype(F32) * scale).astype(BF))
    restored = jnp.concatenate(pieces, axis=1)
    send_x[...] = dot_nn(both, restored).reshape(NE, CAP, KD).astype(BF)

    def scatter(src, dst, n):
        def one_peer(i, _):
            peer = lax.rem(me + i, NE)
            send(src.at[peer], dst.at[me], s_a2a.at[n], r_a2a.at[n], (dp, peer))
            return 0

        lax.fori_loop(1, NE, one_peer, 0)
        dst[me] = src[me]

    def arrived(dst, n):
        wait_for(r_a2a.at[n], got_x.at[pl.ds(0, NE - 1)])
        return dst[...].astype(F32).reshape(ROWS, KD).astype(BF)

    scatter(send_x, got_x, 0)

    small = jnp.concatenate(
        [targets[0], targets[1], gate_ref[...], jnp.zeros((4, TOK), F32)], axis=0
    )
    columns = jnp.concatenate([small, jnp.zeros((8, 256 - TOK), F32)], axis=1).T[:TOK]
    gate0, gate1 = columns[:, 2:3], columns[:, 3:4]
    cot = cot_ref[...].astype(F32)
    sent = dot_nn(hits_t[0], (gate0 * cot).astype(BF)) + dot_nn(hits_t[1], (gate1 * cot).astype(BF))
    send_g[...] = sent.reshape(NE, CAP, KD).astype(BF)
    scatter(send_g, got_g, 1)
    row_lanes = lax.broadcasted_iota(jnp.int32, (TOK, ROWS), 1)
    for k in range(2):
        hits[k] = jnp.where(columns[:, k:k + 1].astype(jnp.int32) == row_lanes, 1.0, 0.0).astype(BF)

    def slabs_of(buf, u):
        some = [buf[16 * z:16 * z + 16][4 * u:4 * u + 4] for z in range(2)]
        some = jnp.concatenate(some, axis=0).astype(F32)
        return some.reshape(NY, SH, KD).astype(BF)

    def xg1(u):
        xg[u, x] = slabs_of(got_x, u)
        for other in (xr, xl):
            send(xg.at[u, x], xg.at[u, x], s_xg1.at[u], m_xg1.at[u], at_x(other))

    def xg2(u):
        wait_for(m_xg1.at[u], xg.at[u, pl.ds(0, 2)])
        lower, upper = xg.at[u, xl, pl.ds(0, 2)], xg.at[u, xr, pl.ds(2, 2)]
        send(lower, lower, s_xg2.at[u], m_xg2.at[u], at_x(xr))
        send(upper, upper, s_xg2.at[u], m_xg2.at[u], at_x(xl))

    def add(*terms):
        total = terms[0].astype(F32)
        for term in terms[1:]:
            total = total + term.astype(F32)
        return total

    def forward_part(u):
        wait_for(m_xg2.at[u], xg.at[u, 0])
        for half in range(2):
            out = None
            for i in range(NX):
                term = dot_nn(xg[u, i].reshape(UR, KD), wx[i, half])
                out = term if out is None else out + term
            pf[u, :, :, FX * half:FX * half + FX] = out.astype(BF).reshape(NY, SH, FX)

    def f1(u):
        send(pf.at[u, y3], fb.at[u, 1], s_f1, m_f1.at[u], at_y(y1))
        send(pf.at[u, y1], fb.at[u, 0], s_f1, m_f1.at[u], at_y(y1))

    def f2(u):
        wait_for(m_f1.at[u], fb.at[u])
        pf[u, y2] = add(pf[u, y2], fb[u, 1]).astype(BF)
        send(pf.at[u, y2], fc.at[u], s_f2, m_f2.at[u], at_y(y2))

    def make_hidden(u):
        wait_for(m_f2.at[u], fc.at[u])
        total = add(pf[u, y], fb[u, 0], fc[u])
        gu_keep[u] = total
        gate, up = total[:, :FX], total[:, FX:]
        hid[u // 2, x, y, u % 2] = ((gate * jax.nn.sigmoid(gate)) * up).astype(BF)

    def backward_part(d):
        for uu in range(2):
            gs[d, :, uu] = slabs_of(got_g, 2 * d + uu)
        left = gs[d].reshape(2 * UR, KD)
        for i in range(NX):
            out = dot_nt(left, dn_ref[FX * i:FX * i + FX, :]).astype(BF)
            pv[d, i] = out.reshape(NY, 2, SH, FX)

    def x1(d):
        send(pv.at[d, xo, pl.ds(0, 2)], r1.at[d, 0], s_x1, m_x1.at[d], at_x(xr))
        send(pv.at[d, xo, pl.ds(2, 2)], r1.at[d, 1], s_x1, m_x1.at[d], at_x(xl))

    def x2_plain(d):
        send(pv.at[d, xr, pl.ds(2, 2)], r2.at[d, 0, pl.ds(2, 2)], s_x2, m_x2.at[d], at_x(xr))
        send(pv.at[d, xl, pl.ds(0, 2)], r2.at[d, 1, pl.ds(0, 2)], s_x2, m_x2.at[d], at_x(xl))

    def x2_added(d):
        wait_for(m_x1.at[d], r1.at[d])
        lower, upper = pl.ds(0, 2), pl.ds(2, 2)
        pv[d, xr, lower] = add(pv[d, xr, lower], r1[d, 0]).astype(BF)
        send(pv.at[d, xr, lower], r2.at[d, 0, lower], s_x2, m_x2.at[d], at_x(xr))
        pv[d, xl, upper] = add(pv[d, xl, upper], r1[d, 1]).astype(BF)
        send(pv.at[d, xl, upper], r2.at[d, 1, upper], s_x2, m_x2.at[d], at_x(xl))

    def v1(d):
        wait_for(m_x2.at[d], r2.at[d])
        qv[d] = add(pv[d, x], r2[d, 0], r2[d, 1]).astype(BF)
        send(qv.at[d, y3], vb.at[d, 1], s_v1, m_v1.at[d], at_y(y1))
        send(qv.at[d, y1], vb.at[d, 0], s_v1, m_v1.at[d], at_y(y1))

    def v2(d):
        wait_for(m_v1.at[d], vb.at[d])
        qv[d, y2] = add(qv[d, y2], vb[d, 1]).astype(BF)
        send(qv.at[d, y2], vc.at[d], s_v2, m_v2.at[d], at_y(y2))

    def make_act(d):
        wait_for(m_v2.at[d], vc.at[d])
        total = add(qv[d, y], vb[d, 0], vc[d])
        for uu in range(2):
            u = 2 * d + uu
            grad = total[uu]
            gate, up = gu_keep[u, :, :FX], gu_keep[u, :, FX:]
            sig = jax.nn.sigmoid(gate)
            act[u, x, y, :, :FX] = (grad * up * sig * (1.0 + gate * (1.0 - sig))).astype(BF)
            act[u, x, y, :, FX:] = (grad * (gate * sig)).astype(BF)

    def unit(a):
        return hid.at[a] if a < ND else act.at[a - ND]

    def ya1(a):
        block = unit(a).at[x, y]
        send(block, block, s_ya1.at[a], m_ya1.at[a], at_y(y2))
        send(block, block, s_ya2.at[a], m_ya2.at[a], at_y(y1))

    def ya2(a):
        block = unit(a).at[x, y2]
        wait_for(m_ya1.at[a], block)
        send(block, block, s_ya2.at[a], m_ya2.at[a], at_y(y1))

    def xa1(a):
        wait_for(m_ya2.at[a], unit(a).at[0, pl.ds(0, 2)])
        mine = unit(a).at[x]
        for other in (xr, xl):
            send(mine, mine, s_xa1.at[a], m_xa1.at[a], at_x(other))

    def xa2(a):
        wait_for(m_xa1.at[a], unit(a).at[pl.ds(0, 2)])
        lower, upper = unit(a).at[xl, pl.ds(0, 2)], unit(a).at[xr, pl.ds(2, 2)]
        send(lower, lower, s_xa2.at[a], m_xa2.at[a], at_x(xr))
        send(upper, upper, s_xa2.at[a], m_xa2.at[a], at_x(xl))

    def gathered(a):
        wait_for(m_xa2.at[a], unit(a).at[0])

    def send_unit(src, dst, u, n, rows_out):
        slabs = rows_out.reshape(8, CAP, KD).astype(BF)
        for z in range(2):
            src[16 * z + 4 * u:16 * z + 4 * u + 4] = slabs[4 * z:4 * z + 4]

        def one_peer(i, _):
            k = lax.rem(me + i, 8)
            peer = 16 * lax.div(k, 4) + 4 * u + lax.rem(k, 4)

            @pl.when(peer != me)
            def _():
                send(src.at[peer], dst.at[me], s_a2a.at[n], r_a2a.at[n], (dp, peer))

            return 0

        lax.fori_loop(0, 8, one_peer, 0)

    def use_hidden(d):
        gathered(d)
        out = None
        for i in range(NX):
            term = dot_nn(hid[d, i].reshape(2 * UR, FX), dn_ref[FX * i:FX * i + FX, :])
            out = term if out is None else out + term
        out = out.reshape(NY, 2, SH, KD)
        for uu in range(2):
            send_unit(send_o, got_o, 2 * d + uu, 2, out[:, uu].reshape(UR, KD))

    def hidden_weights(i):
        grads = dot_nn(gt[...], hid[:, i].reshape(ROWS, FX))
        dg_ref[FX * i:FX * i + FX, :] = grads.T.astype(BF)

    def use_act(u):
        gathered(ND + u)
        out = None
        for i in range(NX):
            for half in range(2):
                term = dot_nt(
                    act[u, i, :, :, FX * half:FX * half + FX].reshape(UR, FX),
                    w_ref[:, half * FF + FX * i:half * FF + FX * i + FX],
                )
                out = term if out is None else out + term
        send_unit(send_i, got_i, u, 3, out)

    def act_weights(d):
        for i in range(NX):
            for half in range(2):
                cols = slice(half * FF + FX * i, half * FF + FX * i + FX)
                right = act[2 * d:2 * d + 2, i, :, :, FX * half:FX * half + FX]
                grads = dot_nn(xt[d], right.reshape(2 * UR, FX))
                if d == 0:
                    gu_acc[:, cols] = grads
                else:
                    gu_ref[:, cols] = (gu_acc[:, cols] + grads).astype(BF)

    wait_for(r_a2a.at[0], got_x.at[pl.ds(0, NE - 1)])
    for u in range(NU):
        xg1(u)
    for copy in keep:
        copy.wait()
    wait_for(m_w, wx.at[pl.ds(0, NX - 1)])
    xg2(0)
    xg2(1)
    forward_part(0)
    f1(0)
    xg2(2)
    forward_part(1)
    f1(1)
    xg2(3)
    f2(0)
    fetch_dn.wait()
    wait_for(r_a2a.at[1], got_x.at[pl.ds(0, NE - 1)])
    backward_part(0)
    x1(0)
    x2_plain(0)
    forward_part(2)
    f1(2)
    f2(1)
    backward_part(1)
    x1(1)
    forward_part(3)
    f1(3)
    make_hidden(0)
    x2_added(0)
    x2_plain(1)
    make_hidden(1)
    ya1(0)
    f2(2)
    x2_added(1)
    f2(3)
    ya2(0)
    make_hidden(2)
    v1(0)
    make_hidden(3)
    ya1(1)
    xa1(0)
    v1(1)
    v2(0)
    ya2(1)
    v2(1)
    make_act(0)
    ya1(2)
    ya1(3)
    xa1(1)
    xa2(0)
    make_act(1)
    ya1(4)
    ya1(5)
    ya2(2)
    ya2(3)
    xa2(1)
    xa1(2)
    ya2(4)
    ya2(5)
    xa1(3)
    use_hidden(0)
    xa2(2)
    xa1(4)
    use_hidden(1)
    xa2(3)
    xa1(5)
    for d in range(ND):
        xt[d] = xg[2 * d:2 * d + 2, x].reshape(2 * UR, KD).T
    gt[...] = gs[...].reshape(ROWS, KD).T
    fetch_w.wait()
    use_act(0)
    xa2(4)
    for i in range(NX):
        hidden_weights(i)
    put_dg = pltpu.make_async_copy(dg_ref, dg_hbm, s_local.at[2])
    put_dg.start()
    use_act(1)
    xa2(5)
    act_weights(0)

    got_o[me] = send_o[me]
    back = arrived(got_o, 2)
    p0, p1 = dot_nn(hits[0], back), dot_nn(hits[1], back)
    lo_ref[...] = (gate0 * p0 + gate1 * p1).astype(BF)
    ones = jnp.ones((8, KD), F32)

    def lane_sums(values):
        return lax.dot_general(
            ones, values, (((1,), (1,)), ((), ())),
            precision=lax.Precision.HIGHEST, preferred_element_type=F32,
        )

    cot_again = cot_ref[...].astype(F32)
    first = lax.broadcasted_iota(jnp.int32, (8, TOK), 0) == 0
    gx[x] = jnp.where(first, lane_sums(cot_again * p0), lane_sums(cot_again * p1))
    for j, other in enumerate((xr, xo, xl)):
        send(gx.at[x], gx.at[x], s_gate.at[0, j], m_gate.at[0, x], at_x(other))
    use_act(2)
    for other in (xr, xo, xl):
        wait_for(m_gate.at[0, other], gx.at[other])
    gy[y] = (gx[0] + gx[1]) + (gx[2] + gx[3])
    for j in (1, 2, 3):
        send(gy.at[y], gy.at[y], s_gate.at[1, j - 1], m_gate.at[1, y], at_y(lax.rem(y + j, NY)))
    use_act(3)
    act_weights(1)
    put_gu = pltpu.make_async_copy(gu_ref, gu_hbm, s_local.at[3])
    put_gu.start()
    for j in (1, 2, 3):
        other = lax.rem(y + j, NY)
        wait_for(m_gate.at[1, other], gy.at[other])
    gg_ref[...] = ((gy[0] + gy[1]) + (gy[2] + gy[3]))[0:2]

    for n, buf in enumerate((send_x, send_g, send_o)):
        wait_for(s_a2a.at[n], buf.at[pl.ds(0, NE - 1)])
    wait_for(s_w, wx.at[pl.ds(0, NX - 1)])
    for u in range(NU):
        wait_for(s_xg1.at[u], xg.at[u, pl.ds(0, 2)])
        wait_for(s_xg2.at[u], xg.at[u, 0])
    wait_for(s_f1, fb)
    wait_for(s_f2, fc)
    wait_for(s_x1, r1)
    wait_for(s_x2, r2)
    wait_for(s_v1, vb)
    wait_for(s_v2, vc)
    for a in range(ND + NU):
        wait_for(s_ya1.at[a], unit(a).at[0, 0])
        wait_for(s_ya2.at[a], unit(a).at[0, pl.ds(0, 2)])
        wait_for(s_xa1.at[a], unit(a).at[pl.ds(0, 2)])
        wait_for(s_xa2.at[a], unit(a).at[0])
    for j in range(3):
        wait_for(s_gate.at[0, j], gx.at[0])
        wait_for(s_gate.at[1, j], gy.at[0])
    put_dg.wait()

    got_i[me] = send_i[me]
    back = arrived(got_i, 3)
    pair = dot_nn(hits[0], back) + dot_nn(hits[1], back)
    high = pair.astype(BF)
    low = (pair - high.astype(F32)).astype(BF)
    for b in range(KD // HB):
        cols = slice(b * HB, (b + 1) * HB)
        out = dot_nn(high[:, cols], signs[...]) + dot_nn(low[:, cols], signs[...])
        tg_ref[:, cols] = (out * (HB ** -0.5)).astype(BF)
    wait_for(s_a2a.at[3], send_x.at[pl.ds(0, NE - 1)])
    put_gu.wait()


def place_results(*refs):
    count = 5
    sources, targets, held = refs[:count], refs[count:2 * count], refs[2 * count:3 * count]
    s_in, s_out = refs[3 * count:]
    order = (3, 4, 0, 1, 2)
    fetch = {n: pltpu.make_async_copy(sources[n], held[n], s_in.at[n]) for n in order}
    put = {n: pltpu.make_async_copy(held[n], targets[n], s_out.at[n]) for n in order}
    for n in order:
        fetch[n].start()
    for n in order:
        fetch[n].wait()
        put[n].start()
    for n in order:
        put[n].wait()


def per_device(tokens, cotangent, expert_ids, gate_values, gate_up_weight, down_weight):
    vmem = pl.BlockSpec(memory_space=pltpu.VMEM)
    hbm = pl.BlockSpec(memory_space=pl.ANY)
    slabs = pltpu.VMEM((NE, CAP, KD), BF)
    dma = pltpu.SemaphoreType.DMA
    results = (
        jax.ShapeDtypeStruct((TOK, KD), BF),
        jax.ShapeDtypeStruct((TOK, KD), BF),
        jax.ShapeDtypeStruct((2, TOK), F32),
        jax.ShapeDtypeStruct((KD, 2 * FF), BF),
        jax.ShapeDtypeStruct((FF, KD), BF),
    )
    made = pl.pallas_call(
        kernel,
        out_shape=results,
        in_specs=[vmem] * 4 + [hbm] * 2,
        out_specs=[vmem] * 3 + [hbm] * 2,
        scratch_shapes=[
            pltpu.VMEM((KD, 2 * FF), BF), pltpu.VMEM((FF, KD), BF),
            pltpu.VMEM((KD, 2 * FF), BF), pltpu.VMEM((FF, KD), BF),
            pltpu.VMEM((KD, 2 * FF), F32), pltpu.VMEM((HB, HB), BF),
            pltpu.VMEM((NX, 2, KD, FX), BF),
            slabs, slabs, slabs, slabs, slabs, slabs, slabs, slabs,
            pltpu.VMEM((NU, NX, NY, SH, KD), BF),
            pltpu.VMEM((ND, NY, 2, SH, KD), BF),
            pltpu.VMEM((ND, KD, 2 * UR), BF), pltpu.VMEM((KD, ROWS), BF),
            pltpu.VMEM((2, TOK, ROWS), BF), pltpu.VMEM((2, ROWS, TOK), BF),
            pltpu.VMEM((NU, NY, SH, 2 * FX), BF),
            pltpu.VMEM((NU, 2, SH, 2 * FX), BF),
            pltpu.VMEM((NU, SH, 2 * FX), BF),
            pltpu.VMEM((ND, NX, NY, 2, SH, FX), BF),
            pltpu.VMEM((ND, 2, 2, 2, SH, FX), BF),
            pltpu.VMEM((ND, 2, NY, 2, SH, FX), BF),
            pltpu.VMEM((ND, NY, 2, SH, FX), BF),
            pltpu.VMEM((ND, 2, 2, SH, FX), BF),
            pltpu.VMEM((ND, 2, SH, FX), BF),
            pltpu.VMEM((NU, SH, 2 * FX), F32),
            pltpu.VMEM((ND, NX, NY, 2, SH, FX), BF),
            pltpu.VMEM((NU, NX, NY, SH, 2 * FX), BF),
            pltpu.VMEM((NX, 8, TOK), F32), pltpu.VMEM((NY, 8, TOK), F32),
            dma((6,)), dma((4,)), dma((4,)),
            dma, dma, dma((NU,)), dma((NU,)), dma((NU,)), dma((NU,)),
            dma, dma, dma((NU,)), dma((NU,)),
            dma, dma, dma((ND,)), dma((ND,)),
            dma, dma, dma((ND,)), dma((ND,)),
            dma((ND + NU,)), dma((ND + NU,)), dma((ND + NU,)), dma((ND + NU,)),
            dma((ND + NU,)), dma((ND + NU,)), dma((ND + NU,)), dma((ND + NU,)),
            dma((2, 3)), dma((2, 4)),
        ],
        compiler_params=pltpu.CompilerParams(
            collective_id=0, has_side_effects=True, vmem_limit_bytes=56 * 1024 * 1024
        ),
        cost_estimate=pl.CostEstimate(
            flops=2 * ROWS * KD * 9 * FF, bytes_accessed=6 * 1024 * 1024, transcendentals=ROWS * FF
        ),
    )(
        tokens, cotangent, expert_ids.T, gate_values.T, gate_up_weight[0], down_weight[0],
    )
    lo, tg, gg, gu, dg = pl.pallas_call(
        place_results,
        out_shape=results,
        in_specs=[hbm] * 5,
        out_specs=[hbm] * 5,
        scratch_shapes=[pltpu.VMEM(r.shape, r.dtype) for r in results] + [dma((5,)), dma((5,))],
    )(*made)
    return lo, tg, gg.T, gu[None], dg[None]


def solution(mesh):
    return jax.shard_map(
        per_device,
        mesh=mesh,
        in_specs=(
            P("expert", "dp"),
            P("expert", "dp"),
            P("expert", None),
            P("expert", None),
            P("expert", "dp", None),
            P("expert", None, "dp"),
        ),
        out_specs=(
            P("expert", "dp"),
            P("expert", "dp"),
            P("expert", None),
            P("expert", "dp", None),
            P("expert", None, "dp"),
        ),
        check_vma=False,
    )
```

time: 143 us -> 125 us (0.87)
  the two profiles are of different devices: /device:TPU:1 before, /device:TPU:64 now
where the time goes in v3:
time: 125 us; the launch traced here: 124 us
  Pallas kernels  124 us (99%)
    pallas_call x1, Pallas kernels, per_device(): pl.pallas_call(kernel, out_shape=results, in_specs=[vmem] * 4 + [hbm] * 2...  121 us
    pallas_call x1, Pallas kernels, per_device(): pl.pallas_call(place_results, out_shape=results, in_specs=[hbm] * 5, out_...  2.51 us

profile of v3, /device:TPU:64, one launch (start us, length us, event | category | flops | bytes accessed | tf_op | source)
XLA Modules:
  0.0 124.3 jit_solution(1465386596710488636)
XLA Ops:
  0.6 121.2 %shard_map.101 = (bf16[192,256]{1,0:T(8,128)(2,1)}, bf16[192,256]{1,0:T(8,128)(2,1)}, f32[2,192]{1,0:T(2,128)}, bf16[256,2048]{1,0:T(8,128)(2,1)}, bf16[1024,256]{1,0:T(8,128)(2,1)}) custom-call(bf16[192,256]{1,0:T(8,128)(2,1)} %tok_ref.1, bf16[192,256]{1,0:T(8,128)(2,1)} %cot_ref.1, s32[2,192]{1,0:T(2,128)} %bitcast.11, f32[2,192]{1,0:T(2,128)} %bitcast.12, ...), custom_call_target="tpu_custom_call" | custom-call | flops 3623878656 | bytes 6291456 | tf_op jit(solution)/shard_map/pallas_call | solution.py:527
  121.8 2.5 %shard_map.102 = (bf16[192,256]{1,0:T(8,128)(2,1)}, bf16[192,256]{1,0:T(8,128)(2,1)}, f32[2,192]{1,0:T(2,128)}, bf16[256,2048]{1,0:T(8,128)(2,1)}, bf16[1024,256]{1,0:T(8,128)(2,1)}) custom-call(bf16[192,256]{1,0:T(8,128)(2,1)} %get-tuple-element.15.refs_0_, bf16[192,256]{1,0:T(8,128)(2,1)} %get-tuple-element.16.refs_1_, ...), custom_call_target="tpu_custom_call" | custom-call | tf_op jit(solution)/shard_map/pallas_call | solution.py:573

commit v4 on v3

--- a/solution.py
+++ b/solution.py
@@ -24,6 +24,7 @@
 UR = ROWS // NU
 SH = UR // NY
 ND = 2
+NEAR = ((0, 28), (4, 24), (12, 16), (8, 20))
 
 
 def dot_nn(a, b):
@@ -147,16 +148,22 @@
     send_x[...] = dot_nn(both, restored).reshape(NE, CAP, KD).astype(BF)
 
     def scatter(src, dst, n):
-        def one_peer(i, _):
-            peer = lax.rem(me + i, NE)
-            send(src.at[peer], dst.at[me], s_a2a.at[n], r_a2a.at[n], (dp, peer))
-            return 0
-
-        lax.fori_loop(1, NE, one_peer, 0)
-        dst[me] = src[me]
+        for u in range(NU):
+            for base in NEAR[u]:
+
+                def one_peer(i, _):
+                    peer = lax.rem(me + i, NE)
+                    send(src.at[peer], dst.at[i], s_a2a.at[n], r_a2a.at[n, u], (dp, peer))
+                    return 0
+
+                lax.fori_loop(max(base, 1), base + 4, one_peer, 0)
+        dst[0] = src[me]
+
+    def wait_unit(n, u):
+        wait_for(r_a2a.at[n, u], got_x.at[pl.ds(0, 7 if u == 0 else 8)])
 
     def arrived(dst, n):
-        wait_for(r_a2a.at[n], got_x.at[pl.ds(0, NE - 1)])
+        wait_for(r_a2a.at[n, 0], got_x.at[pl.ds(0, NE - 1)])
         return dst[...].astype(F32).reshape(ROWS, KD).astype(BF)
 
     scatter(send_x, got_x, 0)
@@ -175,11 +182,11 @@
         hits[k] = jnp.where(columns[:, k:k + 1].astype(jnp.int32) == row_lanes, 1.0, 0.0).astype(BF)
 
     def slabs_of(buf, u):
-        some = [buf[16 * z:16 * z + 16][4 * u:4 * u + 4] for z in range(2)]
-        some = jnp.concatenate(some, axis=0).astype(F32)
+        some = jnp.concatenate([buf[base:base + 4] for base in NEAR[u]], axis=0).astype(F32)
         return some.reshape(NY, SH, KD).astype(BF)
 
     def xg1(u):
+        wait_unit(0, u)
         xg[u, x] = slabs_of(got_x, u)
         for other in (xr, xl):
             send(xg.at[u, x], xg.at[u, x], s_xg1.at[u], m_xg1.at[u], at_x(other))
@@ -223,6 +230,7 @@
 
     def backward_part(d):
         for uu in range(2):
+            wait_unit(1, 2 * d + uu)
             gs[d, :, uu] = slabs_of(got_g, 2 * d + uu)
         left = gs[d].reshape(2 * UR, KD)
         for i in range(NX):
@@ -297,20 +305,15 @@
 
     def send_unit(src, dst, u, n, rows_out):
         slabs = rows_out.reshape(8, CAP, KD).astype(BF)
-        for z in range(2):
-            src[16 * z + 4 * u:16 * z + 4 * u + 4] = slabs[4 * z:4 * z + 4]
-
-        def one_peer(i, _):
-            k = lax.rem(me + i, 8)
-            peer = 16 * lax.div(k, 4) + 4 * u + lax.rem(k, 4)
-
-            @pl.when(peer != me)
-            def _():
-                send(src.at[peer], dst.at[me], s_a2a.at[n], r_a2a.at[n], (dp, peer))
-
-            return 0
-
-        lax.fori_loop(0, 8, one_peer, 0)
+        for z, base in enumerate(NEAR[u]):
+            src[base:base + 4] = slabs[4 * z:4 * z + 4]
+
+            def one_peer(i, _):
+                peer = lax.rem(me + NE - i, NE)
+                send(src.at[i], dst.at[me], s_a2a.at[n], r_a2a.at[n, 0], (dp, peer))
+                return 0
+
+            lax.fori_loop(max(base, 1), base + 4, one_peer, 0)
 
     def use_hidden(d):
         gathered(d)
@@ -349,110 +352,117 @@
                 else:
                     gu_ref[:, cols] = (gu_acc[:, cols] + grads).astype(BF)
 
-    wait_for(r_a2a.at[0], got_x.at[pl.ds(0, NE - 1)])
-    for u in range(NU):
-        xg1(u)
+    def tokens_out():
+        got_o[me] = send_o[0]
+        back = arrived(got_o, 2)
+        p0, p1 = dot_nn(hits[0], back), dot_nn(hits[1], back)
+        lo_ref[...] = (gate0 * p0 + gate1 * p1).astype(BF)
+        ones = jnp.ones((8, KD), F32)
+
+        def lane_sums(values):
+            return lax.dot_general(
+                ones, values, (((1,), (1,)), ((), ())),
+                precision=lax.Precision.HIGHEST, preferred_element_type=F32,
+            )
+
+        cot_again = cot_ref[...].astype(F32)
+        first = lax.broadcasted_iota(jnp.int32, (8, TOK), 0) == 0
+        gx[x] = jnp.where(first, lane_sums(cot_again * p0), lane_sums(cot_again * p1))
+        for j, other in enumerate((xr, xo, xl)):
+            send(gx.at[x], gx.at[x], s_gate.at[0, j], m_gate.at[0, x], at_x(other))
+
+    def gate_pass():
+        for other in (xr, xo, xl):
+            wait_for(m_gate.at[0, other], gx.at[other])
+        gy[y] = (gx[0] + gx[1]) + (gx[2] + gx[3])
+        for j in (1, 2, 3):
+            send(gy.at[y], gy.at[y], s_gate.at[1, j - 1], m_gate.at[1, y], at_y(lax.rem(y + j, NY)))
+
+    xg1(0)
+    xg1(1)
+    xg2(0)
+    xg1(3)
+    xg2(1)
     for copy in keep:
         copy.wait()
     wait_for(m_w, wx.at[pl.ds(0, NX - 1)])
-    xg2(0)
-    xg2(1)
     forward_part(0)
     f1(0)
-    xg2(2)
+    xg2(3)
+    xg1(2)
     forward_part(1)
     f1(1)
-    xg2(3)
     f2(0)
+    forward_part(3)
+    f1(3)
+    xg2(2)
     fetch_dn.wait()
-    wait_for(r_a2a.at[1], got_x.at[pl.ds(0, NE - 1)])
     backward_part(0)
     x1(0)
-    x2_plain(0)
+    f2(1)
     forward_part(2)
     f1(2)
-    f2(1)
+    x2_plain(0)
+    f2(3)
+    make_hidden(0)
+    x2_added(0)
+    make_hidden(1)
+    ya1(0)
     backward_part(1)
     x1(1)
-    forward_part(3)
-    f1(3)
-    make_hidden(0)
-    x2_added(0)
+    f2(2)
     x2_plain(1)
-    make_hidden(1)
-    ya1(0)
-    f2(2)
-    x2_added(1)
-    f2(3)
-    ya2(0)
-    make_hidden(2)
     v1(0)
     make_hidden(3)
+    ya2(0)
+    x2_added(1)
+    make_hidden(2)
     ya1(1)
+    v2(0)
     xa1(0)
+    ya2(1)
     v1(1)
-    v2(0)
-    ya2(1)
+    make_act(0)
+    xa1(1)
+    ya1(3)
     v2(1)
-    make_act(0)
     ya1(2)
-    ya1(3)
-    xa1(1)
     xa2(0)
-    make_act(1)
-    ya1(4)
-    ya1(5)
-    ya2(2)
-    ya2(3)
-    xa2(1)
-    xa1(2)
-    ya2(4)
-    ya2(5)
-    xa1(3)
-    use_hidden(0)
-    xa2(2)
-    xa1(4)
-    use_hidden(1)
-    xa2(3)
-    xa1(5)
     for d in range(ND):
         xt[d] = xg[2 * d:2 * d + 2, x].reshape(2 * UR, KD).T
     gt[...] = gs[...].reshape(ROWS, KD).T
+    ya2(3)
+    xa2(1)
+    make_act(1)
+    xa1(3)
+    ya2(2)
+    ya1(4)
+    xa1(2)
+    ya1(5)
+    ya2(4)
+    use_hidden(1)
+    xa2(3)
+    xa1(4)
+    ya2(5)
+    xa2(2)
     fetch_w.wait()
+    use_act(1)
+    use_hidden(0)
+    xa1(5)
+    hidden_weights(0)
+    hidden_weights(1)
     use_act(0)
     xa2(4)
-    for i in range(NX):
-        hidden_weights(i)
+    hidden_weights(2)
+    hidden_weights(3)
+    act_weights(0)
+    xa2(5)
+    use_act(2)
+    use_act(3)
+    tokens_out()
     put_dg = pltpu.make_async_copy(dg_ref, dg_hbm, s_local.at[2])
     put_dg.start()
-    use_act(1)
-    xa2(5)
-    act_weights(0)
-
-    got_o[me] = send_o[me]
-    back = arrived(got_o, 2)
-    p0, p1 = dot_nn(hits[0], back), dot_nn(hits[1], back)
-    lo_ref[...] = (gate0 * p0 + gate1 * p1).astype(BF)
-    ones = jnp.ones((8, KD), F32)
-
-    def lane_sums(values):
-        return lax.dot_general(
-            ones, values, (((1,), (1,)), ((), ())),
-            precision=lax.Precision.HIGHEST, preferred_element_type=F32,
-        )
-
-    cot_again = cot_ref[...].astype(F32)
-    first = lax.broadcasted_iota(jnp.int32, (8, TOK), 0) == 0
-    gx[x] = jnp.where(first, lane_sums(cot_again * p0), lane_sums(cot_again * p1))
-    for j, other in enumerate((xr, xo, xl)):
-        send(gx.at[x], gx.at[x], s_gate.at[0, j], m_gate.at[0, x], at_x(other))
-    use_act(2)
-    for other in (xr, xo, xl):
-        wait_for(m_gate.at[0, other], gx.at[other])
-    gy[y] = (gx[0] + gx[1]) + (gx[2] + gx[3])
-    for j in (1, 2, 3):
-        send(gy.at[y], gy.at[y], s_gate.at[1, j - 1], m_gate.at[1, y], at_y(lax.rem(y + j, NY)))
-    use_act(3)
+    gate_pass()
     act_weights(1)
     put_gu = pltpu.make_async_copy(gu_ref, gu_hbm, s_local.at[3])
     put_gu.start()
@@ -483,7 +493,7 @@
         wait_for(s_gate.at[1, j], gy.at[0])
     put_dg.wait()
 
-    got_i[me] = send_i[me]
+    got_i[me] = send_i[0]
     back = arrived(got_i, 3)
     pair = dot_nn(hits[0], back) + dot_nn(hits[1], back)
     high = pair.astype(BF)
@@ -552,7 +562,7 @@
             pltpu.VMEM((ND, NX, NY, 2, SH, FX), BF),
             pltpu.VMEM((NU, NX, NY, SH, 2 * FX), BF),
             pltpu.VMEM((NX, 8, TOK), F32), pltpu.VMEM((NY, 8, TOK), F32),
-            dma((6,)), dma((4,)), dma((4,)),
+            dma((6,)), dma((4,)), dma((4, NU)),
             dma, dma, dma((NU,)), dma((NU,)), dma((NU,)), dma((NU,)),
             dma, dma, dma((NU,)), dma((NU,)),
             dma, dma, dma((ND,)), dma((ND,)),

time: 125 us -> 115 us (0.920)
  the two profiles are of different devices: /device:TPU:64 before, /device:TPU:1 now
where the time goes in v4:
time: 115 us
  Pallas kernels  114 us (99%)
    pallas_call x1, Pallas kernels, per_device(): pl.pallas_call(kernel, out_shape=results, in_specs=[vmem] * 4 + [hbm] * 2...  112 us
    pallas_call x1, Pallas kernels, per_device(): pl.pallas_call(place_results, out_shape=results, in_specs=[hbm] * 5, out_...  2.51 us

profile of v4, /device:TPU:1, one launch (start us, length us, event | category | flops | bytes accessed | tf_op | source)
XLA Modules:
  0.0 114.9 jit_solution(12287269617947170131)
XLA Ops:
  0.6 111.8 %shard_map.101 = (bf16[192,256]{1,0:T(8,128)(2,1)}, bf16[192,256]{1,0:T(8,128)(2,1)}, f32[2,192]{1,0:T(2,128)}, bf16[256,2048]{1,0:T(8,128)(2,1)}, bf16[1024,256]{1,0:T(8,128)(2,1)}) custom-call(bf16[192,256]{1,0:T(8,128)(2,1)} %tok_ref.1, bf16[192,256]{1,0:T(8,128)(2,1)} %cot_ref.1, s32[2,192]{1,0:T(2,128)} %bitcast.11, f32[2,192]{1,0:T(2,128)} %bitcast.12, ...), custom_call_target="tpu_custom_call" | custom-call | flops 3623878656 | bytes 6291456 | tf_op jit(solution)/shard_map/pallas_call | solution.py:537
  112.4 2.5 %shard_map.102 = (bf16[192,256]{1,0:T(8,128)(2,1)}, bf16[192,256]{1,0:T(8,128)(2,1)}, f32[2,192]{1,0:T(2,128)}, bf16[256,2048]{1,0:T(8,128)(2,1)}, bf16[1024,256]{1,0:T(8,128)(2,1)}) custom-call(bf16[192,256]{1,0:T(8,128)(2,1)} %get-tuple-element.15.refs_0_, bf16[192,256]{1,0:T(8,128)(2,1)} %get-tuple-element.16.refs_1_, ...), custom_call_target="tpu_custom_call" | custom-call | tf_op jit(solution)/shard_map/pallas_call | solution.py:583

commit v5 on v4

--- a/solution.py
+++ b/solution.py
@@ -506,20 +506,27 @@
     put_gu.wait()
 
 
+PIECES = tuple((3, r, 64) for r in range(0, KD, 64)) + tuple((4, r, 256) for r in range(0, FF, 256)) + (
+    (0, 0, TOK), (1, 0, TOK), (2, 0, 2)
+)
+
+
 def place_results(*refs):
     count = 5
     sources, targets, held = refs[:count], refs[count:2 * count], refs[2 * count:3 * count]
     s_in, s_out = refs[3 * count:]
-    order = (3, 4, 0, 1, 2)
-    fetch = {n: pltpu.make_async_copy(sources[n], held[n], s_in.at[n]) for n in order}
-    put = {n: pltpu.make_async_copy(held[n], targets[n], s_out.at[n]) for n in order}
-    for n in order:
-        fetch[n].start()
-    for n in order:
-        fetch[n].wait()
-        put[n].start()
-    for n in order:
-        put[n].wait()
+    fetch, put = [], []
+    for k, (n, row, size) in enumerate(PIECES):
+        rows = pl.ds(row, size)
+        fetch.append(pltpu.make_async_copy(sources[n].at[rows], held[n].at[rows], s_in.at[k]))
+        put.append(pltpu.make_async_copy(held[n].at[rows], targets[n].at[rows], s_out.at[k]))
+    for copy in fetch:
+        copy.start()
+    for k in range(len(PIECES)):
+        fetch[k].wait()
+        put[k].start()
+    for copy in put:
+        copy.wait()
 
 
 def per_device(tokens, cotangent, expert_ids, gate_values, gate_up_weight, down_weight):
@@ -585,7 +592,7 @@
         out_shape=results,
         in_specs=[hbm] * 5,
         out_specs=[hbm] * 5,
-        scratch_shapes=[pltpu.VMEM(r.shape, r.dtype) for r in results] + [dma((5,)), dma((5,))],
+        scratch_shapes=[pltpu.VMEM(r.shape, r.dtype) for r in results] + [dma((len(PIECES),)), dma((len(PIECES),))],
     )(*made)
     return lo, tg, gg.T, gu[None], dg[None]
 

time: 115 us -> 115 us (level)
  no operation moved by 1% of the time
where the time goes in v5:
time: 115 us
  Pallas kernels  114 us (99%)
    pallas_call x1, Pallas kernels, per_device(): pl.pallas_call(kernel, out_shape=results, in_specs=[vmem] * 4 + [hbm] * 2...  112 us
    pallas_call x1, Pallas kernels, per_device(): pl.pallas_call(place_results, out_shape=results, in_specs=[hbm] * 5, out_...  2.34 us

profile of v5, /device:TPU:1, one launch (start us, length us, event | category | flops | bytes accessed | tf_op | source)
XLA Modules:
  0.0 114.8 jit_solution(1000981268739749066)
XLA Ops:
  0.6 111.8 %shard_map.101 = (bf16[192,256]{1,0:T(8,128)(2,1)}, bf16[192,256]{1,0:T(8,128)(2,1)}, f32[2,192]{1,0:T(2,128)}, bf16[256,2048]{1,0:T(8,128)(2,1)}, bf16[1024,256]{1,0:T(8,128)(2,1)}) custom-call(bf16[192,256]{1,0:T(8,128)(2,1)} %tok_ref.1, bf16[192,256]{1,0:T(8,128)(2,1)} %cot_ref.1, s32[2,192]{1,0:T(2,128)} %bitcast.11, f32[2,192]{1,0:T(2,128)} %bitcast.12, ...), custom_call_target="tpu_custom_call" | custom-call | flops 3623878656 | bytes 6291456 | tf_op jit(solution)/shard_map/pallas_call | solution.py:544
  112.4 2.3 %shard_map.102 = (bf16[192,256]{1,0:T(8,128)(2,1)}, bf16[192,256]{1,0:T(8,128)(2,1)}, f32[2,192]{1,0:T(2,128)}, bf16[256,2048]{1,0:T(8,128)(2,1)}, bf16[1024,256]{1,0:T(8,128)(2,1)}) custom-call(bf16[192,256]{1,0:T(8,128)(2,1)} %get-tuple-element.15.refs_0_, bf16[192,256]{1,0:T(8,128)(2,1)} %get-tuple-element.16.refs_1_, ...), custom_call_target="tpu_custom_call" | custom-call | tf_op jit(solution)/shard_map/pallas_call | solution.py:590
